TPU v7x, 512 devices: a whole 4x8x8 slice. The times are simulated.
512 devices in a mesh: tm: 128 (over x, z, y_hi, core), panel: 4 (over y_lo).
Axes of the slice: x: 4, y: 8 (y_hi: 2, y_lo: 4; y = y_hi * 4 + y_lo), z: 8, core: 2. Of those that a mesh axis runs over, the one named last changes fastest.
Arguments:
- forward_props: bfloat16 [2, 128, 1024, 1024], P(None, 'tm', 'panel'), may hold values from -2 to 2
Outputs:
- prefix_props: bfloat16 [2, 128, 1024, 1024], P(None, 'tm', 'panel')
All inputs are finite; a program needn't handle non-finite values.
Results may differ from a plain program's by a relative error of at most 0.0057.
Values may be sent and summed in bfloat16 or wider, within the bound.
A program may use at most 64 MiB of HBM per device.

v0:
```python
import jax
import jax.numpy as jnp
from jax import lax
from jax.sharding import PartitionSpec as P

SECTIONS = 2


def shifted(x, axis, by):
    size = lax.axis_size(axis)
    pairs = [(i, i + by) for i in range(size) if 0 <= i + by < size]
    return lax.ppermute(x, axis, pairs)


def complex_rows(left, right):
    real_part = jnp.dot(left[0], right[0], preferred_element_type=jnp.float32) - jnp.dot(
        left[1], right[1], preferred_element_type=jnp.float32
    )
    imag_part = jnp.dot(left[0], right[1], preferred_element_type=jnp.float32) + jnp.dot(
        left[1], right[0], preferred_element_type=jnp.float32
    )
    return (real_part, imag_part)


def shards(forward_props):
    chain = forward_props[:, 0]
    position = lax.axis_index("tm")
    for level in range(SECTIONS):
        distance = 2**level
        whole = lax.all_gather(chain, "panel", axis=1, tiled=True)
        earlier = shifted(whole, "tm", distance)
        real_part, imag_part = complex_rows(chain, earlier)
        product = jnp.stack([real_part, imag_part]).astype(jnp.bfloat16)
        chain = jnp.where(position >= distance, product, chain)
    return chain[:, None]


def solution(mesh):
    placed = (P(None, "tm", "panel", None),)
    return jax.shard_map(
        shards, mesh=mesh, in_specs=placed, out_specs=P(None, "tm", "panel", None), check_vma=False
    )
```

profile of v0, /device:TPU:7, one launch (start us, length us, event | category | flops | bytes accessed | tf_op | source)
XLA Modules:
  0.0 506.6 jit_solution(5649751116792492340)
XLA Ops:
  6.5 0.0 copy-start
  6.5 0.0 all-gather.6.cloned.1.call-start
  6.5 0.7 all-gather.6.cloned.1.call-update
  7.3 0.0 all-gather.4.cloned.1.call-start
  7.3 93.4 %all-gather.6.cloned.1.call-done = bf16[2,1,1024,1024]{3,2,1,0:T(8,128)(2,1)} async-done(((bf16[2,1,256,1024]{3,2,1,0:T(8,128)(2,1)}), bf16[2,1,1024,1024]{3,2,1,0:T(8,128)(2,1)}) %all-gather.6.cloned.1.call-update) | async-done | bytes 4194320 | tf_op jit(solution)/shard_map/all_gather | solution.py:30
  100.7 6.2 %collective-permute-start = (bf16[2,1024,1024]{2,1,0:T(8,128)(2,1)}, bf16[2,1024,1024]{2,1,0:T(8,128)(2,1)}, u32[]{:S(2)}, u32[]{:S(2)}) collective-permute-start(bf16[2,1024,1024]{2,1,0:T(8,128)(2,1)} %bitcast.69), channel_id=1, source_target_pairs={{0,4},{4,8},{8,12},{12,16},{16,20},{20,24},{24,28},{28,32},{32,36}... | collective-permute-start | bytes 12582920 | tf_op jit(solution)/shard_map/ppermute | solution.py:12
  107.0 67.9 %collective-permute-done = bf16[2,1024,1024]{2,1,0:T(8,128)(2,1)} collective-permute-done((bf16[2,1024,1024]{2,1,0:T(8,128)(2,1)}, bf16[2,1024,1024]{2,1,0:T(8,128)(2,1)}, u32[]{:S(2)}, u32[]{:S(2)}) %collective-permute-start) | collective-permute-done | bytes 4194336 | tf_op jit(solution)/shard_map/ppermute | solution.py:12
  174.8 2.5 fusion
  177.3 0.0 copy-done
  177.3 2.3 fusion.3
  179.6 2.3 fusion.13
  182.0 2.3 fusion.12
  184.3 1.1 maximum_select_fusion
  185.4 0.0 copy-start.1
  185.4 0.0 all-gather.4.cloned.1.call-update
  185.4 111.8 %all-gather.4.cloned.1.call-done = bf16[2,1024,1024]{2,1,0:T(8,128)(2,1)} async-done(((bf16[2,256,1024]{2,1,0:T(8,128)(2,1)}), bf16[2,1024,1024]{2,1,0:T(8,128)(2,1)}) %all-gather.4.cloned.1.call-update) | async-done | bytes 4194320 | tf_op jit(solution)/shard_map/all_gather | solution.py:30
  297.2 5.9 %collective-permute-start.1 = (bf16[2,1024,1024]{2,1,0:T(8,128)(2,1)}, bf16[2,1024,1024]{2,1,0:T(8,128)(2,1)}, u32[]{:S(2)}, u32[]{:S(2)}) collective-permute-start(bf16[2,1024,1024]{2,1,0:T(8,128)(2,1)} %all-gather.4.cloned.1.call-done), channel_id=1, source_target_pairs={{0,8},{4,12},{8,16},{12,20},{16,24},{20,28},{24,32},{28,36},{32,40... | collective-permute-start | bytes 12582920 | tf_op jit(solution)/shard_map/ppermute | solution.py:12
  303.1 186.1 %collective-permute-done.1 = bf16[2,1024,1024]{2,1,0:T(8,128)(2,1)} collective-permute-done((bf16[2,1024,1024]{2,1,0:T(8,128)(2,1)}, bf16[2,1024,1024]{2,1,0:T(8,128)(2,1)}, u32[]{:S(2)}, u32[]{:S(2)}) %collective-permute-start.1) | collective-permute-done | bytes 4194336 | tf_op jit(solution)/shard_map/ppermute | solution.py:12
  489.1 2.5 fusion.4
  491.6 0.0 copy-done.1
  491.6 2.3 fusion.7
  493.9 2.3 fusion.16
  496.2 2.3 fusion.17
  498.6 1.2 maximum_select_fusion.1
Async XLA Ops:
  6.5 170.8 %copy-start = (bf16[2,1,256,1024]{3,2,1,0:T(8,128)(2,1)S(1)}, bf16[2,1,256,1024]{3,2,1,0:T(8,128)(2,1)}, u32[]{:S(2)}) copy-start(bf16[2,1,256,1024]{3,2,1,0:T(8,128)(2,1)} %param.1) | copy-start | bytes 3145732
  6.5 94.2 %all-gather.6.cloned.1.call-start = ((), (), s32[]{:S(2)}) async-start(), calls=%async_computation.1 | async-start | bytes 5242880 | tf_op jit(solution)/shard_map/all_gather | solution.py:30
  7.3 289.9 %all-gather.4.cloned.1.call-start = ((), (), s32[]{:S(2)}) async-start(), calls=%async_computation | async-start | bytes 5242880 | tf_op jit(solution)/shard_map/all_gather | solution.py:30
  100.7 74.1 %collective-permute-start = (bf16[2,1024,1024]{2,1,0:T(8,128)(2,1)}, bf16[2,1024,1024]{2,1,0:T(8,128)(2,1)}, u32[]{:S(2)}, u32[]{:S(2)}) collective-permute-start(bf16[2,1024,1024]{2,1,0:T(8,128)(2,1)} %bitcast.69), channel_id=1, source_target_pairs={{0,4},{4,8},{8,12},{12,16},{16,20},{20,24},{24,28},{28,32},{32,36}... | collective-permute-start | bytes 12582920 | tf_op jit(solution)/shard_map/ppermute | solution.py:12
  185.4 306.2 %copy-start.1 = (bf16[2,256,1024]{2,1,0:T(8,128)(2,1)S(1)}, bf16[2,256,1024]{2,1,0:T(8,128)(2,1)}, u32[]{:S(2)}) copy-start(bf16[2,256,1024]{2,1,0:T(8,128)(2,1)} %maximum_select_fusion) | copy-start | bytes 3145732
  297.2 191.9 %collective-permute-start.1 = (bf16[2,1024,1024]{2,1,0:T(8,128)(2,1)}, bf16[2,1024,1024]{2,1,0:T(8,128)(2,1)}, u32[]{:S(2)}, u32[]{:S(2)}) collective-permute-start(bf16[2,1024,1024]{2,1,0:T(8,128)(2,1)} %all-gather.4.cloned.1.call-done), channel_id=1, source_target_pairs={{0,8},{4,12},{8,16},{12,20},{16,24},{20,28},{24,32},{28,36},{32,40... | collective-permute-start | bytes 12582920 | tf_op jit(solution)/shard_map/ppermute | solution.py:12
Sparse Core Ops, SparseCore 0:
  9.5 91.2 all-gather.5
  185.5 111.5 all-gather.3
where the time goes:
time: 508 us; the launch traced here: 507 us
  waiting for transfers between devices  460 us (91%)
  matrix products  18.8 us (4%)
  between operations  13.5 us (3%)
  starting transfers between devices  12.1 us (2%)
    ppermute x2, waiting for transfers between devices, shifted(): return lax.ppermute(x, axis, pairs)  254 us
    all_gather x2, waiting for transfers between devices, shards(): whole = lax.all_gather(chain, 'panel', axis=1, tiled=True)  205 us
    ppermute x2, starting transfers between devices, shifted(): return lax.ppermute(x, axis, pairs)  12.1 us
  transfers between devices with their start and end apart: 4, of which 4 were waited for; matrix products, arithmetic and copies ran while one was open for 0% of the time, Pallas kernels for 0%

commit v1 on v0

v1 whole, which is shorter than its diff:
```python
import functools

import jax
import jax.numpy as jnp
from jax import lax
from jax.experimental import pallas as pl
from jax.experimental.pallas import tpu as pltpu
from jax.sharding import PartitionSpec as P

PANELS = 4
CHUNKS = 8
BANDS = 4

bf16, f32 = jnp.bfloat16, jnp.float32


def dot(a, b):
    return jnp.dot(a, b, preferred_element_type=f32)


def when(cond):
    return pl.when(cond)


def loop(n, body):
    def step(i, carry):
        body(i)
        return carry

    lax.fori_loop(0, n, step, 0)


def kernel(
    tm_size, x_ref, out_ref, own, obuf, o2buf, ebuf, dsend, drecv, dloc, gbuf, acc,
    in_sem, o_recv, o_right, o_left, o_z, o2_recv, e_recv, e_right, e_left, e_in, d_recv, d_out, d_in,
):
    rows, width = x_ref.shape[1], x_ref.shape[2]
    cols = width // CHUNKS
    band = rows // BANDS
    tm, p = lax.axis_index("tm"), lax.axis_index("panel")
    core = lax.rem(tm, 2)
    site = tm // 2

    def at(shift, panel):
        return (lax.rem(tm + shift + tm_size, tm_size), panel)

    def remote(src, dst, send, recv, where):
        return pltpu.make_async_remote_copy(
            src_ref=src, dst_ref=dst, send_sem=send, recv_sem=recv,
            device_id=where, device_id_type=pl.DeviceIdType.MESH,
        )

    def o_rows(q, c):
        return pl.ds(pl.multiple_of(q * rows + c * band, band), band)

    def o_copy(q, c, sems, where, dst=None, recv=None):
        piece = obuf.at[:, o_rows(q, c), :]
        target = piece if dst is None else dst.at[:, o_rows(q, c), :]
        arrive = (o_recv if recv is None else recv).at[q, c]
        return remote(piece, target, sems.at[q, c], arrive, where)

    def o_r(q, c):
        return o_copy(q, c, o_right, at(0, lax.rem(p + 1, PANELS)))

    def o_l(q, c):
        return o_copy(q, c, o_left, at(0, lax.rem(p + PANELS - 1, PANELS)))

    def o_up(q, c):
        return o_copy(q, c, o_z, at(3, p), o2buf, o2_recv)

    def e_piece(q, j):
        return ebuf.at[j, :, pl.ds(pl.multiple_of(q * rows, rows), rows), :]

    def e_copy(q, j, sems, panel):
        return remote(e_piece(q, j), e_piece(q, j), sems.at[q, j], e_recv.at[q, j], at(0, panel))

    def e_r(q, j):
        return e_copy(q, j, e_right, lax.rem(p + 1, PANELS))

    def e_l(q, j):
        return e_copy(q, j, e_left, lax.rem(p + PANELS - 1, PANELS))

    def e_over(j):
        columns = pl.ds(pl.multiple_of(j * cols, cols), cols)
        return remote(own.at[:, :, columns], e_piece(p, j), e_in.at[j], e_recv.at[p, j], at(1, p))

    def d_next(j):
        return remote(dsend.at[j], drecv.at[j], d_out.at[j], d_recv.at[j], at(1, PANELS - 1 - p))

    def d_pass(j, panel):
        return remote(drecv.at[j], drecv.at[j], d_out.at[j], d_recv.at[j], at(0, panel))

    def d_over(j):
        return remote(drecv.at[j], drecv.at[j], d_in.at[j], d_recv.at[j], at(1, p))

    edge = (p == 0) | (p == PANELS - 1)
    low = p < PANELS // 2

    def arrival(i):
        inner = jnp.where(i < 4, jnp.where(lax.rem(i, 2) == 0, i // 2, 7 - i // 2), i - 2)
        a = jnp.where(edge, i, inner)
        j = jnp.where(low, a, CHUNKS - 1 - a)
        return a, j

    load = pltpu.make_async_copy(x_ref, own, in_sem)
    load.start()

    barrier = pltpu.get_barrier_semaphore()

    def greet(where):
        pl.semaphore_signal(barrier, inc=1, device_id=where, device_id_type=pl.DeviceIdType.MESH)

    @when(p > 0)
    def _():
        greet(at(0, p - 1))

    @when(p < PANELS - 1)
    def _():
        greet(at(0, p + 1))

    @when(core == 0)
    def _():
        greet(at(1, p))
        greet(at(-3, p))

        @when(edge)
        def _():
            greet(at(-1, PANELS - 1 - p))

    @when(core == 1)
    def _():
        greet(at(-1, p))
        greet(at(3, p))

        @when(edge)
        def _():
            greet(at(1, PANELS - 1 - p))

    load.wait()
    pl.semaphore_wait(barrier, 4)

    @when(core == 0)
    def _():
        loop(CHUNKS, lambda j: e_over(j).start())
        acc[...] = jnp.zeros_like(acc)

        def gather_o2(i):
            q, c = i // BANDS, lax.rem(i, BANDS)
            o_copy(q, c, o_z, at(-3, p), o2buf, o2_recv).wait_recv()

        loop(PANELS * BANDS, gather_o2)

        def step(i):
            a, j = arrival(i)
            d_over(j).wait_recv()

            @when((p == 0) & (a < 6))
            def _():
                d_pass(j, 1).start()

            @when((p == 3) & (a < 6))
            def _():
                d_pass(j, 2).start()

            @when((p == 1) & (a < 2))
            def _():
                d_pass(j, 2).start()

            @when((p == 2) & (a < 2))
            def _():
                d_pass(j, 1).start()

            d_over(j).start()
            columns = pl.ds(pl.multiple_of(j * cols, cols), cols)
            er, ei = own[0], own[1]
            dr, di = drecv[j, 0], drecv[j, 1]
            gr = (dot(er, dr) - dot(ei, di)).astype(bf16)
            gi = (dot(er, di) + dot(ei, dr)).astype(bf16)
            gbuf[0, :, columns] = gr
            gbuf[1, :, columns] = gi
            tr, ti = o2buf[0, columns, :], o2buf[1, columns, :]
            acc[0] += dot(gr, tr) - dot(gi, ti)
            acc[1] += dot(gr, ti) + dot(gi, tr)

        loop(CHUNKS, step)
        out_ref[...] = jnp.where(site == 0, own[...], jnp.where(site == 1, gbuf[...], acc[...].astype(bf16)))

        def drain(i):
            a, j = arrival(i)
            e_over(i).wait_send()
            d_over(j).wait_send()

            @when(a < jnp.where(edge, 6, 2))
            def _():
                d_pass(j, 1).wait_send()

        loop(CHUNKS, drain)

    @when(core == 1)
    def _():
        obuf[:, pl.ds(pl.multiple_of(p * rows, rows), rows), :] = own[...]

        def pass_o(q, c, right, left):
            @when(right & (p < PANELS - 1))
            def _():
                o_r(q, c).start()

            @when(left & (p > 0))
            def _():
                o_l(q, c).start()

            o_up(q, c).start()

        loop(BANDS, lambda c: pass_o(p, c, True, True))

        def hop(n):
            def one(c):
                @when(p - 1 - n >= 0)
                def _():
                    o_r(p - 1 - n, c).wait_recv()
                    pass_o(p - 1 - n, c, True, False)

                @when(p + 1 + n < PANELS)
                def _():
                    o_l(p + 1 + n, c).wait_recv()
                    pass_o(p + 1 + n, c, False, True)

            loop(BANDS, one)

        def own_e():
            loop(CHUNKS, lambda j: e_over(j).wait_recv())

        hop(0)
        own_e()

        @when(p == 0)
        def _():
            loop(CHUNKS, lambda j: e_r(0, j).start())

        @when(p == 3)
        def _():
            loop(CHUNKS, lambda j: e_l(3, CHUNKS - 1 - j).start())

        hop(1)

        @when(p == 1)
        def _():
            def one(j):
                e_r(1, j).start()
                e_r(0, j).wait_recv()
                e_r(0, j).start()

            loop(CHUNKS, one)

        @when(p == 2)
        def _():
            def one(i):
                j = CHUNKS - 1 - i
                e_l(2, j).start()
                e_l(3, j).wait_recv()
                e_l(3, j).start()

            loop(CHUNKS, one)

        hop(2)

        @when(p == 1)
        def _():
            loop((PANELS - 1) * BANDS, lambda i: o_l(1 + i // BANDS, lax.rem(i, BANDS)).wait_send())

            def one(i):
                j = CHUNKS - 1 - i
                e_l(1, j).start()
                e_l(2, j).wait_recv()
                e_l(2, j).start()
                e_l(3, j).wait_recv()
                e_l(3, j).start()

            loop(CHUNKS, one)
            loop(CHUNKS, lambda j: e_r(0, j).wait_send())

        @when(p == 2)
        def _():
            loop((PANELS - 1) * BANDS, lambda i: o_r(i // BANDS, lax.rem(i, BANDS)).wait_send())

            def one(j):
                e_r(2, j).start()
                e_r(1, j).wait_recv()
                e_r(1, j).start()
                e_r(0, j).wait_recv()
                e_r(0, j).start()

            loop(CHUNKS, one)
            loop(CHUNKS, lambda j: e_l(3, j).wait_send())

        def product(q, j):
            here = pl.ds(pl.multiple_of(q * rows, rows), rows)
            ar, ai = obuf[0, here, :], obuf[1, here, :]
            br, bi = ebuf[j, 0], ebuf[j, 1]
            re = (dot(ar, br) - dot(ai, bi)).astype(bf16)
            im = (dot(ar, bi) + dot(ai, br)).astype(bf16)
            return re, im

        @when(edge)
        def _():
            def one(i):
                j = jnp.where(p == 0, CHUNKS - 1 - i, i)

                @when(p == 0)
                def _():
                    loop(PANELS - 1, lambda q: e_l(q + 1, j).wait_recv())

                @when(p == 3)
                def _():
                    loop(PANELS - 1, lambda q: e_r(q, j).wait_recv())

                def block(q):
                    here = pl.ds(pl.multiple_of(q * rows, rows), rows)
                    re, im = product(q, j)
                    dsend[j, 0, here, :] = re
                    dsend[j, 1, here, :] = im

                loop(PANELS, block)
                d_next(j).start()
                mine = pl.ds(pl.multiple_of(p * rows, rows), rows)
                columns = pl.ds(pl.multiple_of(j * cols, cols), cols)
                dloc[:, :, columns] = dsend[j, :, mine, :]

            loop(CHUNKS, one)

        @when(p == 1)
        def _():
            loop(CHUNKS, lambda j: e_l(2, j).wait_send())

        @when(~edge)
        def _():
            def one(j):
                columns = pl.ds(pl.multiple_of(j * cols, cols), cols)
                re, im = product(p, j)
                dloc[0, :, columns] = re
                dloc[1, :, columns] = im

            loop(CHUNKS, one)

        def step(i):
            _, j = arrival(i)
            d_over(j).wait_recv()
            columns = pl.ds(pl.multiple_of(j * cols, cols), cols)
            ar, ai = dloc[0], dloc[1]
            br, bi = drecv[j, 0], drecv[j, 1]
            re = (dot(ar, br) - dot(ai, bi)).astype(bf16)
            im = (dot(ar, bi) + dot(ai, br)).astype(bf16)
            out_ref[0, :, columns] = jnp.where(site == 0, dloc[0, :, columns], re)
            out_ref[1, :, columns] = jnp.where(site == 0, dloc[1, :, columns], im)

        loop(CHUNKS, step)

        def drain_o(i):
            q, c = i // BANDS, lax.rem(i, BANDS)
            o_up(q, c).wait_send()

            @when((q <= p) & (p < PANELS - 1) & (p != 2))
            def _():
                o_r(q, c).wait_send()

            @when((q >= p) & (p > 0) & (p != 1))
            def _():
                o_l(q, c).wait_send()

        loop(PANELS * BANDS, drain_o)

        def drain_e(j):
            @when(p == 0)
            def _():
                e_r(0, j).wait_send()

            @when(p == 3)
            def _():
                e_l(3, j).wait_send()

            @when(p == 1)
            def _():
                e_r(1, j).wait_send()
                e_l(1, j).wait_send()
                e_l(3, j).wait_send()

            @when(p == 2)
            def _():
                e_l(2, j).wait_send()
                loop(PANELS - 1, lambda q: e_r(q, j).wait_send())

            @when(edge)
            def _():
                d_next(j).wait_send()

        loop(CHUNKS, drain_e)


def shards(forward_props):
    x = forward_props[:, 0]
    _, rows, width = x.shape
    cols = width // CHUNKS
    dma = pltpu.SemaphoreType.DMA
    tm_size = lax.axis_size("tm")
    out = pl.pallas_call(
        functools.partial(kernel, tm_size),
        out_shape=jax.ShapeDtypeStruct(x.shape, bf16),
        in_specs=[pl.BlockSpec(memory_space=pl.ANY)],
        out_specs=pl.BlockSpec(memory_space=pltpu.VMEM),
        scratch_shapes=[
            pltpu.VMEM(x.shape, bf16),
            pltpu.VMEM((2, width, width), bf16),
            pltpu.VMEM((2, width, width), bf16),
            pltpu.VMEM((CHUNKS, 2, width, cols), bf16),
            pltpu.VMEM((CHUNKS, 2, width, cols), bf16),
            pltpu.VMEM((CHUNKS, 2, width, cols), bf16),
            pltpu.VMEM(x.shape, bf16),
            pltpu.VMEM(x.shape, bf16),
            pltpu.VMEM(x.shape, f32),
            dma,
            dma((PANELS, BANDS)),
            dma((PANELS, BANDS)),
            dma((PANELS, BANDS)),
            dma((PANELS, BANDS)),
            dma((PANELS, BANDS)),
            dma((PANELS, CHUNKS)),
            dma((PANELS, CHUNKS)),
            dma((PANELS, CHUNKS)),
            dma((CHUNKS,)),
            dma((CHUNKS,)),
            dma((CHUNKS,)),
            dma((CHUNKS,)),
        ],
        compiler_params=pltpu.CompilerParams(
            collective_id=0, has_side_effects=True, vmem_limit_bytes=48 * 2**20
        ),
        name="prefix_products",
    )(x)
    return out[:, None]


def solution(mesh):
    placed = (P(None, "tm", "panel", None),)
    return jax.shard_map(
        shards, mesh=mesh, in_specs=placed, out_specs=P(None, "tm", "panel", None), check_vma=False
    )
```

time: 508 us -> 150 us (0.30)
  the two profiles are of different devices: /device:TPU:7 before, /device:TPU:17 now
where the time goes in v1:
time: 150 us
  Pallas kernels  148 us (99%)
  local copies, waits for them, and re-layouts  2.2 us (1%)
    pallas_call x1, Pallas kernels, shards(): pl.pallas_call(functools.partial(kernel, tm_size), out_shape=jax.ShapeDty...  148 us

profile of v1, /device:TPU:17, one launch (start us, length us, event | category | flops | bytes accessed | tf_op | source)
XLA Modules:
  0.0 150.1 jit_solution(11139077569435857245)
XLA Ops:
  0.0 0.0 copy-start
  0.0 1.2 copy-done
  1.2 147.9 %prefix_products.1 = bf16[2,256,1024]{2,1,0:T(8,128)(2,1)S(1)} custom-call(bf16[2,256,1024]{2,1,0:T(8,128)(2,1)S(1)} %bitcast.5), custom_call_target="tpu_custom_call" | custom-call | tf_op jit(solution)/shard_map/prefix_products/pallas_call | solution.py:405
  149.1 1.0 copy.4
Async XLA Ops:
  0.0 1.2 copy-start

commit v2 on v1

--- a/solution.py
+++ b/solution.py
@@ -9,6 +9,7 @@
 
 PANELS = 4
 CHUNKS = 8
+WINDOW = 2
 BANDS = 4
 
 bf16, f32 = jnp.bfloat16, jnp.float32
@@ -97,11 +98,20 @@
     low = p < PANELS // 2
 
     def arrival(i):
-        inner = jnp.where(i < 4, jnp.where(lax.rem(i, 2) == 0, i // 2, 7 - i // 2), i - 2)
-        a = jnp.where(edge, i, inner)
+        inner = jnp.where(i < 2, i, jnp.where(i == 2, 7, jnp.where(i == 3, 2, jnp.where(i == 4, 6, i - 2))))
+        outer = jnp.where(i < 6, i, 13 - i)
+        a = jnp.where(edge, outer, inner)
         j = jnp.where(low, a, CHUNKS - 1 - a)
         return a, j
 
+    def passes(a):
+        return jnp.where(edge, a < 6, (a < 2) | (a == 7))
+
+    def pass_to(a):
+        onward = jnp.where(edge, jnp.where(low, 1, 2), jnp.where(low, 2, 1))
+        back = jnp.where(low, 0, PANELS - 1)
+        return jnp.where(~edge & (a == 7), back, onward)
+
     load = pltpu.make_async_copy(x_ref, own, in_sem)
     load.start()
 
@@ -120,7 +130,6 @@
 
     @when(core == 0)
     def _():
-        greet(at(1, p))
         greet(at(-3, p))
 
         @when(edge)
@@ -130,59 +139,57 @@
     @when(core == 1)
     def _():
         greet(at(-1, p))
-        greet(at(3, p))
-
-        @when(edge)
-        def _():
-            greet(at(1, PANELS - 1 - p))
 
     load.wait()
-    pl.semaphore_wait(barrier, 4)
+    pl.semaphore_wait(barrier, jnp.where((core == 0) & edge, 2, 3))
 
     @when(core == 0)
     def _():
         loop(CHUNKS, lambda j: e_over(j).start())
         acc[...] = jnp.zeros_like(acc)
 
-        def gather_o2(i):
-            q, c = i // BANDS, lax.rem(i, BANDS)
-            o_copy(q, c, o_z, at(-3, p), o2buf, o2_recv).wait_recv()
-
-        loop(PANELS * BANDS, gather_o2)
-
-        def step(i):
+        def take(i):
             a, j = arrival(i)
             d_over(j).wait_recv()
 
-            @when((p == 0) & (a < 6))
-            def _():
-                d_pass(j, 1).start()
-
-            @when((p == 3) & (a < 6))
-            def _():
-                d_pass(j, 2).start()
-
-            @when((p == 1) & (a < 2))
-            def _():
-                d_pass(j, 2).start()
-
-            @when((p == 2) & (a < 2))
-            def _():
-                d_pass(j, 1).start()
+            @when(passes(a))
+            def _():
+                d_pass(j, pass_to(a)).start()
 
             d_over(j).start()
             columns = pl.ds(pl.multiple_of(j * cols, cols), cols)
             er, ei = own[0], own[1]
             dr, di = drecv[j, 0], drecv[j, 1]
-            gr = (dot(er, dr) - dot(ei, di)).astype(bf16)
-            gi = (dot(er, di) + dot(ei, dr)).astype(bf16)
-            gbuf[0, :, columns] = gr
-            gbuf[1, :, columns] = gi
+            gbuf[0, :, columns] = (dot(er, dr) - dot(ei, di)).astype(bf16)
+            gbuf[1, :, columns] = (dot(er, di) + dot(ei, dr)).astype(bf16)
+
+        def add(i):
+            _, j = arrival(i)
+
+            def rows_in(n):
+                o_copy(j // 2, 2 * lax.rem(j, 2) + n, o_z, at(-3, p), o2buf, o2_recv).wait_recv()
+
+            loop(BANDS // 2, rows_in)
+            columns = pl.ds(pl.multiple_of(j * cols, cols), cols)
+            gr, gi = gbuf[0, :, columns], gbuf[1, :, columns]
             tr, ti = o2buf[0, columns, :], o2buf[1, columns, :]
             acc[0] += dot(gr, tr) - dot(gi, ti)
             acc[1] += dot(gr, ti) + dot(gi, tr)
 
+        def added(i):
+            return jnp.where(i < 3, 0, jnp.where(i < 6, 2 * i - 5, i))
+
+        def step(i):
+            take(i)
+
+            def more(n, carry):
+                add(n)
+                return carry
+
+            lax.fori_loop(added(i - 1), added(i), more, 0)
+
         loop(CHUNKS, step)
+        add(CHUNKS - 1)
         out_ref[...] = jnp.where(site == 0, own[...], jnp.where(site == 1, gbuf[...], acc[...].astype(bf16)))
 
         def drain(i):
@@ -190,7 +197,7 @@
             e_over(i).wait_send()
             d_over(j).wait_send()
 
-            @when(a < jnp.where(edge, 6, 2))
+            @when(passes(a))
             def _():
                 d_pass(j, 1).wait_send()
 
@@ -270,6 +277,11 @@
 
             def one(i):
                 j = CHUNKS - 1 - i
+
+                @when(i >= WINDOW)
+                def _():
+                    loop(PANELS - 1, lambda q: e_l(q + 1, j + WINDOW).wait_send())
+
                 e_l(1, j).start()
                 e_l(2, j).wait_recv()
                 e_l(2, j).start()
@@ -277,13 +289,16 @@
                 e_l(3, j).start()
 
             loop(CHUNKS, one)
-            loop(CHUNKS, lambda j: e_r(0, j).wait_send())
 
         @when(p == 2)
         def _():
             loop((PANELS - 1) * BANDS, lambda i: o_r(i // BANDS, lax.rem(i, BANDS)).wait_send())
 
             def one(j):
+                @when(j >= WINDOW)
+                def _():
+                    loop(PANELS - 1, lambda q: e_r(q, j - WINDOW).wait_send())
+
                 e_r(2, j).start()
                 e_r(1, j).wait_recv()
                 e_r(1, j).start()
@@ -291,7 +306,6 @@
                 e_r(0, j).start()
 
             loop(CHUNKS, one)
-            loop(CHUNKS, lambda j: e_l(3, j).wait_send())
 
         def product(q, j):
             here = pl.ds(pl.multiple_of(q * rows, rows), rows)
@@ -321,16 +335,16 @@
                     dsend[j, 1, here, :] = im
 
                 loop(PANELS, block)
-                d_next(j).start()
+
+                @when(i < CHUNKS - 1)
+                def _():
+                    d_next(j).start()
+
                 mine = pl.ds(pl.multiple_of(p * rows, rows), rows)
                 columns = pl.ds(pl.multiple_of(j * cols, cols), cols)
                 dloc[:, :, columns] = dsend[j, :, mine, :]
 
             loop(CHUNKS, one)
-
-        @when(p == 1)
-        def _():
-            loop(CHUNKS, lambda j: e_l(2, j).wait_send())
 
         @when(~edge)
         def _():
@@ -380,16 +394,23 @@
 
             @when(p == 1)
             def _():
+                e_r(0, j).wait_send()
                 e_r(1, j).wait_send()
-                e_l(1, j).wait_send()
+
+                @when(j < WINDOW)
+                def _():
+                    loop(PANELS - 1, lambda q: e_l(q + 1, j).wait_send())
+
+            @when(p == 2)
+            def _():
+                e_l(2, j).wait_send()
                 e_l(3, j).wait_send()
 
-            @when(p == 2)
-            def _():
-                e_l(2, j).wait_send()
-                loop(PANELS - 1, lambda q: e_r(q, j).wait_send())
-
-            @when(edge)
+                @when(j >= CHUNKS - WINDOW)
+                def _():
+                    loop(PANELS - 1, lambda q: e_r(q, j).wait_send())
+
+            @when((p == 0) & (j > 0) | (p == PANELS - 1) & (j < CHUNKS - 1))
             def _():
                 d_next(j).wait_send()
 

time: 150 us -> 109 us (0.73)
  the two profiles are of different devices: /device:TPU:17 before, /device:TPU:9 now
where the time goes in v2:
time: 109 us
  Pallas kernels  107 us (98%)
  local copies, waits for them, and re-layouts  2.2 us (2%)
    pallas_call x1, Pallas kernels, shards(): pl.pallas_call(functools.partial(kernel, tm_size), out_shape=jax.ShapeDty...  107 us
    unnamed x3, local copies, waits for them, and re-layouts  2.2 us

profile of v2, /device:TPU:9, one launch (start us, length us, event | category | flops | bytes accessed | tf_op | source)
XLA Modules:
  0.0 109.1 jit_solution(12305634999887395610)
XLA Ops:
  0.0 0.0 copy-start
  0.0 1.2 %copy-done = bf16[2,1,256,1024]{3,2,1,0:T(8,128)(2,1)S(1)} copy-done((bf16[2,1,256,1024]{3,2,1,0:T(8,128)(2,1)S(1)}, bf16[2,1,256,1024]{3,2,1,0:T(8,128)(2,1)}, u32[]{:S(2)}) %copy-start) | copy-done | bytes 1048600
  1.2 106.9 %prefix_products.1 = bf16[2,256,1024]{2,1,0:T(8,128)(2,1)S(1)} custom-call(bf16[2,256,1024]{2,1,0:T(8,128)(2,1)S(1)} %bitcast.5), custom_call_target="tpu_custom_call" | custom-call | tf_op jit(solution)/shard_map/prefix_products/pallas_call | solution.py:426
  108.1 1.0 copy.4
Async XLA Ops:
  0.0 1.2 %copy-start = (bf16[2,1,256,1024]{3,2,1,0:T(8,128)(2,1)S(1)}, bf16[2,1,256,1024]{3,2,1,0:T(8,128)(2,1)}, u32[]{:S(2)}) copy-start(bf16[2,1,256,1024]{3,2,1,0:T(8,128)(2,1)} %param.1) | copy-start | bytes 3145732

commit v3 on v2

--- a/solution.py
+++ b/solution.py
@@ -9,7 +9,6 @@
 
 PANELS = 4
 CHUNKS = 8
-WINDOW = 2
 BANDS = 4
 
 bf16, f32 = jnp.bfloat16, jnp.float32
@@ -40,7 +39,7 @@
     band = rows // BANDS
     tm, p = lax.axis_index("tm"), lax.axis_index("panel")
     core = lax.rem(tm, 2)
-    site = tm // 2
+    site, sites = tm // 2, tm_size // 2
 
     def at(shift, panel):
         return (lax.rem(tm + shift + tm_size, tm_size), panel)
@@ -94,26 +93,37 @@
     def d_over(j):
         return remote(drecv.at[j], drecv.at[j], d_in.at[j], d_recv.at[j], at(1, p))
 
+    odd = lax.rem(site, 2) == 1
+    direct_out = jnp.where(odd, 6, 7)
+    direct_in = jnp.where(odd, 7, 6)
     edge = (p == 0) | (p == PANELS - 1)
     low = p < PANELS // 2
 
+    def pick(i, values):
+        found = values[-1]
+        for n in range(len(values) - 1):
+            found = jnp.where(i == n, values[n], found)
+        return found
+
     def arrival(i):
-        inner = jnp.where(i < 2, i, jnp.where(i == 2, 7, jnp.where(i == 3, 2, jnp.where(i == 4, 6, i - 2))))
-        outer = jnp.where(i < 6, i, 13 - i)
+        inner = pick(i, (0, 1, 7, 2, 6, 3, 5, 4))
+        outer = jnp.where(odd, pick(i, (0, 1, 2, 3, 4, 7, 5, 6)), pick(i, (0, 1, 2, 3, 4, 7, 6, 5)))
         a = jnp.where(edge, outer, inner)
         j = jnp.where(low, a, CHUNKS - 1 - a)
         return a, j
 
     def passes(a):
-        return jnp.where(edge, a < 6, (a < 2) | (a == 7))
+        return jnp.where(edge, a < 5, (a < 3) | (a >= direct_in))
 
     def pass_to(a):
         onward = jnp.where(edge, jnp.where(low, 1, 2), jnp.where(low, 2, 1))
         back = jnp.where(low, 0, PANELS - 1)
-        return jnp.where(~edge & (a == 7), back, onward)
-
-    load = pltpu.make_async_copy(x_ref, own, in_sem)
-    load.start()
+        return jnp.where(~edge & (a >= direct_in), back, onward)
+
+    load_e = pltpu.make_async_copy(x_ref, own, in_sem)
+    load_o = pltpu.make_async_copy(x_ref, obuf.at[:, pl.ds(pl.multiple_of(p * rows, rows), rows), :], in_sem)
+    when(core == 0)(load_e.start)
+    when(core == 1)(load_o.start)
 
     barrier = pltpu.get_barrier_semaphore()
 
@@ -140,7 +150,8 @@
     def _():
         greet(at(-1, p))
 
-    load.wait()
+    when(core == 0)(load_e.wait)
+    when(core == 1)(load_o.wait)
     pl.semaphore_wait(barrier, jnp.where((core == 0) & edge, 2, 3))
 
     @when(core == 0)
@@ -169,7 +180,10 @@
             def rows_in(n):
                 o_copy(j // 2, 2 * lax.rem(j, 2) + n, o_z, at(-3, p), o2buf, o2_recv).wait_recv()
 
-            loop(BANDS // 2, rows_in)
+            @when(site > 1)
+            def _():
+                loop(BANDS // 2, rows_in)
+
             columns = pl.ds(pl.multiple_of(j * cols, cols), cols)
             gr, gi = gbuf[0, :, columns], gbuf[1, :, columns]
             tr, ti = o2buf[0, columns, :], o2buf[1, columns, :]
@@ -188,25 +202,37 @@
 
             lax.fori_loop(added(i - 1), added(i), more, 0)
 
-        loop(CHUNKS, step)
-        add(CHUNKS - 1)
-        out_ref[...] = jnp.where(site == 0, own[...], jnp.where(site == 1, gbuf[...], acc[...].astype(bf16)))
-
         def drain(i):
             a, j = arrival(i)
-            e_over(i).wait_send()
             d_over(j).wait_send()
 
             @when(passes(a))
             def _():
                 d_pass(j, 1).wait_send()
 
-        loop(CHUNKS, drain)
+        @when(site == 0)
+        def _():
+            out_ref[...] = own[...]
+
+        @when(site > 0)
+        def _():
+            loop(CHUNKS, step)
+            add(CHUNKS - 1)
+
+            @when(site == 1)
+            def _():
+                out_ref[...] = gbuf[...]
+
+            @when(site > 1)
+            def _():
+                out_ref[...] = acc[...].astype(bf16)
+
+            loop(CHUNKS, drain)
+
+        loop(CHUNKS, lambda j: e_over(j).wait_send())
 
     @when(core == 1)
     def _():
-        obuf[:, pl.ds(pl.multiple_of(p * rows, rows), rows), :] = own[...]
-
         def pass_o(q, c, right, left):
             @when(right & (p < PANELS - 1))
             def _():
@@ -216,7 +242,10 @@
             def _():
                 o_l(q, c).start()
 
-            o_up(q, c).start()
+
+            @when(site < sites - 2)
+            def _():
+                o_up(q, c).start()
 
         loop(BANDS, lambda c: pass_o(p, c, True, True))
 
@@ -273,15 +302,8 @@
 
         @when(p == 1)
         def _():
-            loop((PANELS - 1) * BANDS, lambda i: o_l(1 + i // BANDS, lax.rem(i, BANDS)).wait_send())
-
             def one(i):
                 j = CHUNKS - 1 - i
-
-                @when(i >= WINDOW)
-                def _():
-                    loop(PANELS - 1, lambda q: e_l(q + 1, j + WINDOW).wait_send())
-
                 e_l(1, j).start()
                 e_l(2, j).wait_recv()
                 e_l(2, j).start()
@@ -292,13 +314,7 @@
 
         @when(p == 2)
         def _():
-            loop((PANELS - 1) * BANDS, lambda i: o_r(i // BANDS, lax.rem(i, BANDS)).wait_send())
-
             def one(j):
-                @when(j >= WINDOW)
-                def _():
-                    loop(PANELS - 1, lambda q: e_r(q, j - WINDOW).wait_send())
-
                 e_r(2, j).start()
                 e_r(1, j).wait_recv()
                 e_r(1, j).start()
@@ -306,6 +322,9 @@
                 e_r(0, j).start()
 
             loop(CHUNKS, one)
+
+        def nth(i):
+            return jnp.where(p == 0, CHUNKS - 1 - i, i)
 
         def product(q, j):
             here = pl.ds(pl.multiple_of(q * rows, rows), rows)
@@ -318,7 +337,7 @@
         @when(edge)
         def _():
             def one(i):
-                j = jnp.where(p == 0, CHUNKS - 1 - i, i)
+                j = nth(i)
 
                 @when(p == 0)
                 def _():
@@ -336,7 +355,7 @@
 
                 loop(PANELS, block)
 
-                @when(i < CHUNKS - 1)
+                @when((i < direct_out) & (site < sites - 1))
                 def _():
                     d_next(j).start()
 
@@ -364,57 +383,55 @@
             br, bi = drecv[j, 0], drecv[j, 1]
             re = (dot(ar, br) - dot(ai, bi)).astype(bf16)
             im = (dot(ar, bi) + dot(ai, br)).astype(bf16)
-            out_ref[0, :, columns] = jnp.where(site == 0, dloc[0, :, columns], re)
-            out_ref[1, :, columns] = jnp.where(site == 0, dloc[1, :, columns], im)
-
-        loop(CHUNKS, step)
+            out_ref[0, :, columns] = re
+            out_ref[1, :, columns] = im
+
+        @when(site == 0)
+        def _():
+            out_ref[...] = dloc[...]
+
+        @when(site > 0)
+        def _():
+            loop(CHUNKS, step)
 
         def drain_o(i):
             q, c = i // BANDS, lax.rem(i, BANDS)
-            o_up(q, c).wait_send()
-
-            @when((q <= p) & (p < PANELS - 1) & (p != 2))
+
+            @when(site < sites - 2)
+            def _():
+                o_up(q, c).wait_send()
+
+            @when((q <= p) & (p < PANELS - 1))
             def _():
                 o_r(q, c).wait_send()
 
-            @when((q >= p) & (p > 0) & (p != 1))
+            @when((q >= p) & (p > 0))
             def _():
                 o_l(q, c).wait_send()
 
         loop(PANELS * BANDS, drain_o)
 
-        def drain_e(j):
-            @when(p == 0)
-            def _():
-                e_r(0, j).wait_send()
-
-            @when(p == 3)
-            def _():
-                e_l(3, j).wait_send()
-
-            @when(p == 1)
-            def _():
-                e_r(0, j).wait_send()
-                e_r(1, j).wait_send()
-
-                @when(j < WINDOW)
-                def _():
-                    loop(PANELS - 1, lambda q: e_l(q + 1, j).wait_send())
-
-            @when(p == 2)
-            def _():
-                e_l(2, j).wait_send()
-                e_l(3, j).wait_send()
-
-                @when(j >= CHUNKS - WINDOW)
-                def _():
-                    loop(PANELS - 1, lambda q: e_r(q, j).wait_send())
-
-            @when((p == 0) & (j > 0) | (p == PANELS - 1) & (j < CHUNKS - 1))
-            def _():
-                d_next(j).wait_send()
-
-        loop(CHUNKS, drain_e)
+        def drain_e(i):
+            q, j = i // CHUNKS, lax.rem(i, CHUNKS)
+
+            @when((q <= p) & (p < PANELS - 1))
+            def _():
+                e_r(q, j).wait_send()
+
+            @when((q >= p) & (p > 0))
+            def _():
+                e_l(q, j).wait_send()
+
+        loop(PANELS * CHUNKS, drain_e)
+
+        @when(edge)
+        def _():
+            def drain_d(i):
+                @when((i < direct_out) & (site < sites - 1))
+                def _():
+                    d_next(nth(i)).wait_send()
+
+            loop(CHUNKS, drain_d)
 
 
 def shards(forward_props):

time: 109 us -> 103 us (0.945)
  the two profiles are of different devices: /device:TPU:9 before, /device:TPU:7 now
where the time goes in v3:
time: 103 us
  Pallas kernels  101 us (98%)
  local copies, waits for them, and re-layouts  2.2 us (2%)
    pallas_call x1, Pallas kernels, shards(): pl.pallas_call(functools.partial(kernel, tm_size), out_shape=jax.ShapeDty...  101 us
    unnamed x3, local copies, waits for them, and re-layouts  2.2 us

profile of v3, /device:TPU:7, one launch (start us, length us, event | category | flops | bytes accessed | tf_op | source)
XLA Modules:
  0.0 103.1 jit_solution(17759078722979427563)
XLA Ops:
  0.0 0.0 copy-start
  0.0 1.2 %copy-done = bf16[2,1,256,1024]{3,2,1,0:T(8,128)(2,1)S(1)} copy-done((bf16[2,1,256,1024]{3,2,1,0:T(8,128)(2,1)S(1)}, bf16[2,1,256,1024]{3,2,1,0:T(8,128)(2,1)}, u32[]{:S(2)}) %copy-start) | copy-done | bytes 1048600
  1.2 100.9 %prefix_products.1 = bf16[2,256,1024]{2,1,0:T(8,128)(2,1)S(1)} custom-call(bf16[2,256,1024]{2,1,0:T(8,128)(2,1)S(1)} %bitcast.5), custom_call_target="tpu_custom_call" | custom-call | tf_op jit(solution)/shard_map/prefix_products/pallas_call | solution.py:443
  102.1 1.0 copy.4
Async XLA Ops:
  0.0 1.2 %copy-start = (bf16[2,1,256,1024]{3,2,1,0:T(8,128)(2,1)S(1)}, bf16[2,1,256,1024]{3,2,1,0:T(8,128)(2,1)}, u32[]{:S(2)}) copy-start(bf16[2,1,256,1024]{3,2,1,0:T(8,128)(2,1)} %param.1) | copy-start | bytes 3145732

commit v4 on v3

--- a/solution.py
+++ b/solution.py
@@ -9,6 +9,7 @@
 
 PANELS = 4
 CHUNKS = 8
+EARLY = 4
 BANDS = 4
 
 bf16, f32 = jnp.bfloat16, jnp.float32
@@ -33,6 +34,7 @@
 def kernel(
     tm_size, x_ref, out_ref, own, obuf, o2buf, ebuf, dsend, drecv, dloc, gbuf, acc,
     in_sem, o_recv, o_right, o_left, o_z, o2_recv, e_recv, e_right, e_left, e_in, d_recv, d_out, d_in,
+    relay, relay_recv, relay_out, rows_recv, rows_out,
 ):
     rows, width = x_ref.shape[1], x_ref.shape[2]
     cols = width // CHUNKS
@@ -68,6 +70,17 @@
     def o_up(q, c):
         return o_copy(q, c, o_z, at(3, p), o2buf, o2_recv)
 
+    def o_aside(c):
+        here = pl.ds(pl.multiple_of(c * band, band), band)
+        return remote(
+            obuf.at[:, o_rows(p, c), :], relay.at[:, here, :], o_z.at[p, c], relay_recv.at[c], at(5, PANELS - 1 - p)
+        )
+
+    def o_aside_on(c):
+        here = pl.ds(pl.multiple_of(c * band, band), band)
+        q = PANELS - 1 - p
+        return remote(relay.at[:, here, :], o2buf.at[:, o_rows(q, c), :], relay_out.at[c], o2_recv.at[q, c], at(-2, q))
+
     def e_piece(q, j):
         return ebuf.at[j, :, pl.ds(pl.multiple_of(q * rows, rows), rows), :]
 
@@ -92,6 +105,24 @@
 
     def d_over(j):
         return remote(drecv.at[j], drecv.at[j], d_in.at[j], d_recv.at[j], at(1, p))
+
+    def piece(half, g, k, n):
+        first = 2 * g
+        q = jnp.where(half == 0, PANELS - 1 - k, k)
+        j = jnp.where(half == 0, first, CHUNKS - first - n)
+        return pl.ds(j, n), slice(None), pl.ds(pl.multiple_of(q * rows, rows), rows), slice(None)
+
+    def rows_next(half, g, k):
+        view = piece(half, g, k, 2)
+        m = PANELS * g + k
+        return remote(
+            dsend.at[view], drecv.at[view], rows_out.at[half, m], rows_recv.at[half, m], at(1, PANELS - 1 - p)
+        )
+
+    def rows_pass(half, g, k, n, panel):
+        view = piece(half, g, k, n)
+        m = PANELS * g + k
+        return remote(drecv.at[view], drecv.at[view], rows_out.at[half, m], rows_recv.at[half, m], at(0, panel))
 
     odd = lax.rem(site, 2) == 1
     direct_out = jnp.where(odd, 6, 7)
@@ -106,8 +137,8 @@
         return found
 
     def arrival(i):
-        inner = pick(i, (0, 1, 7, 2, 6, 3, 5, 4))
-        outer = jnp.where(odd, pick(i, (0, 1, 2, 3, 4, 7, 5, 6)), pick(i, (0, 1, 2, 3, 4, 7, 6, 5)))
+        inner = jnp.where(odd, pick(i, (0, 1, 7, 2, 6, 3, 5, 4)), pick(i, (0, 1, 2, 3, 7, 6, 5, 4)))
+        outer = pick(i, (0, 1, 2, 3, 4, 7, 6, 5))
         a = jnp.where(edge, outer, inner)
         j = jnp.where(low, a, CHUNKS - 1 - a)
         return a, j
@@ -146,20 +177,40 @@
         def _():
             greet(at(-1, PANELS - 1 - p))
 
+        @when(edge & odd)
+        def _():
+            greet(at(-5, PANELS - 1 - p))
+
+        @when(edge & ~odd)
+        def _():
+            greet(at(2, PANELS - 1 - p))
+
     @when(core == 1)
     def _():
         greet(at(-1, p))
 
     when(core == 0)(load_e.wait)
     when(core == 1)(load_o.wait)
-    pl.semaphore_wait(barrier, jnp.where((core == 0) & edge, 2, 3))
+    pl.semaphore_wait(barrier, jnp.where(edge & ~odd, jnp.where(core == 0, 2, 4), 3))
 
     @when(core == 0)
     def _():
         loop(CHUNKS, lambda j: e_over(j).start())
         acc[...] = jnp.zeros_like(acc)
 
+        @when(edge & odd & (site > 2))
+        def _():
+            def hand_on(c):
+                o_aside(c).wait_recv()
+                o_aside_on(c).start()
+
+            loop(BANDS, hand_on)
+
         def take(i):
+            come(i)
+            multiply(i)
+
+        def come(i):
             a, j = arrival(i)
             d_over(j).wait_recv()
 
@@ -168,27 +219,60 @@
                 d_pass(j, pass_to(a)).start()
 
             d_over(j).start()
+
+        def multiply(i):
+            _, j = arrival(i)
             columns = pl.ds(pl.multiple_of(j * cols, cols), cols)
             er, ei = own[0], own[1]
             dr, di = drecv[j, 0], drecv[j, 1]
             gbuf[0, :, columns] = (dot(er, dr) - dot(ei, di)).astype(bf16)
             gbuf[1, :, columns] = (dot(er, di) + dot(ei, dr)).astype(bf16)
 
-        def add(i):
+        def add(i, final=False):
             _, j = arrival(i)
 
             def rows_in(n):
                 o_copy(j // 2, 2 * lax.rem(j, 2) + n, o_z, at(-3, p), o2buf, o2_recv).wait_recv()
 
-            @when(site > 1)
-            def _():
-                loop(BANDS // 2, rows_in)
-
+            loop(BANDS // 2, rows_in)
             columns = pl.ds(pl.multiple_of(j * cols, cols), cols)
             gr, gi = gbuf[0, :, columns], gbuf[1, :, columns]
             tr, ti = o2buf[0, columns, :], o2buf[1, columns, :]
-            acc[0] += dot(gr, tr) - dot(gi, ti)
-            acc[1] += dot(gr, ti) + dot(gi, tr)
+            re = acc[0] + (dot(gr, tr) - dot(gi, ti))
+            im = acc[1] + (dot(gr, ti) + dot(gi, tr))
+            if final:
+                out_ref[0] = re.astype(bf16)
+                out_ref[1] = im.astype(bf16)
+            else:
+                acc[0] = re
+                acc[1] = im
+
+        def pair_of(g):
+            return jnp.where(low, 2 * g, CHUNKS - 2 - 2 * g)
+
+        def multiply_pair(g):
+            j = pair_of(g)
+            columns = pl.ds(pl.multiple_of(j * cols, cols), 2 * cols)
+            er, ei = own[0], own[1]
+            dr = jnp.concatenate([drecv[j, 0], drecv[j + 1, 0]], axis=1)
+            di = jnp.concatenate([drecv[j, 1], drecv[j + 1, 1]], axis=1)
+            gbuf[0, :, columns] = (dot(er, dr) - dot(ei, di)).astype(bf16)
+            gbuf[1, :, columns] = (dot(er, di) + dot(ei, dr)).astype(bf16)
+
+        def add_pair(g, final=False):
+            j = pair_of(g)
+            loop(BANDS, lambda c: o_copy(j // 2, c, o_z, at(-3, p), o2buf, o2_recv).wait_recv())
+            columns = pl.ds(pl.multiple_of(j * cols, cols), 2 * cols)
+            gr, gi = gbuf[0, :, columns], gbuf[1, :, columns]
+            tr, ti = o2buf[0, columns, :], o2buf[1, columns, :]
+            re = acc[0] + (dot(gr, tr) - dot(gi, ti))
+            im = acc[1] + (dot(gr, ti) + dot(gi, tr))
+            if final:
+                out_ref[0] = re.astype(bf16)
+                out_ref[1] = im.astype(bf16)
+            else:
+                acc[0] = re
+                acc[1] = im
 
         def added(i):
             return jnp.where(i < 3, 0, jnp.where(i < 6, 2 * i - 5, i))
@@ -200,7 +284,9 @@
                 add(n)
                 return carry
 
-            lax.fori_loop(added(i - 1), added(i), more, 0)
+            @when(site > 1)
+            def _():
+                lax.fori_loop(added(i - 1), added(i), more, 0)
 
         def drain(i):
             a, j = arrival(i)
@@ -210,26 +296,113 @@
             def _():
                 d_pass(j, 1).wait_send()
 
+        main = jnp.where(low, 0, 1)
+        other = 1 - main
+
+        def span(first, end, f):
+            loop(end - first, lambda i: f(first + i))
+
+        def take_rows(k):
+            @when(edge)
+            def _():
+                for g in range(2):
+                    rows_pass(main, g, k, 2, pass_to(0)).wait_recv()
+                    rows_pass(main, g, k, 2, pass_to(0)).start()
+
+                @when(k > 0)
+                def _():
+                    rows_pass(other, 0, k - 1, 2, pass_to(0)).wait_recv()
+
+            @when(~edge)
+            def _():
+                for g in range(2):
+                    rows_pass(main, g, k, 2, pass_to(0)).wait_recv()
+                    rows_pass(main, g, k, 2 - g, pass_to(0)).start()
+                for g in range(2):
+                    rows_pass(other, g, k, 2 - g, pass_to(0)).wait_recv()
+                    if g == 0:
+                        rows_pass(other, g, k, 2, pass_to(7)).start()
+
+        def drain_rows(k):
+            rows_pass(main, 0, k, 2, pass_to(0)).wait_send()
+
+            @when(edge)
+            def _():
+                rows_pass(main, 1, k, 2, pass_to(0)).wait_send()
+
+            @when(~edge)
+            def _():
+                rows_pass(main, 1, k, 1, pass_to(0)).wait_send()
+                rows_pass(other, 0, k, 2, pass_to(7)).wait_send()
+
+        def over(i):
+            d_over(arrival(i)[1]).start()
+
         @when(site == 0)
         def _():
             out_ref[...] = own[...]
 
-        @when(site > 0)
+        @when((site > 0) & odd)
         def _():
             loop(CHUNKS, step)
-            add(CHUNKS - 1)
-
-            @when(site == 1)
-            def _():
-                out_ref[...] = gbuf[...]
-
-            @when(site > 1)
-            def _():
-                out_ref[...] = acc[...].astype(bf16)
-
             loop(CHUNKS, drain)
 
+        @when((site > 0) & ~odd)
+        def _():
+            loop(PANELS, take_rows)
+            span(0, 4, over)
+
+            @when(~edge)
+            def _():
+                span(4, 7, over)
+
+            loop(2, multiply_pair)
+
+            @when(edge)
+            def _():
+                come(4)
+                loop(2, add_pair)
+                rows_pass(other, 0, PANELS - 1, 2, pass_to(0)).wait_recv()
+                span(5, 7, over)
+
+            multiply_pair(3)
+
+            @when(~edge)
+            def _():
+                come(7)
+                loop(2, add_pair)
+
+            add_pair(3)
+
+            @when(edge)
+            def _():
+                come(7)
+
+            multiply_pair(2)
+            add_pair(2, final=True)
+
+        @when(site == 1)
+        def _():
+            out_ref[...] = gbuf[...]
+
+        @when((site > 1) & odd)
+        def _():
+            add(CHUNKS - 1, final=True)
+
+        @when((site > 0) & ~odd)
+        def _():
+            loop(PANELS, drain_rows)
+            loop(CHUNKS, lambda j: d_over(j).wait_send())
+
+            @when(edge)
+            def _():
+                d_pass(arrival(4)[1], 1).wait_send()
+
         loop(CHUNKS, lambda j: e_over(j).wait_send())
+
+        @when(edge & odd & (site > 2))
+        def _():
+            loop(BANDS, lambda c: o_aside_on(c).wait_send())
 
     @when(core == 1)
     def _():
@@ -242,12 +415,15 @@
             def _():
                 o_l(q, c).start()
 
-
-            @when(site < sites - 2)
+            aside = edge & ~odd & (q == p)
+
+            @when((site < sites - 2) & ~aside)
             def _():
                 o_up(q, c).start()
 
-        loop(BANDS, lambda c: pass_o(p, c, True, True))
+            @when((site < sites - 2) & aside)
+            def _():
+                o_aside(c).start()
 
         def hop(n):
             def one(c):
@@ -265,63 +441,6 @@
 
         def own_e():
             loop(CHUNKS, lambda j: e_over(j).wait_recv())
-
-        hop(0)
-        own_e()
-
-        @when(p == 0)
-        def _():
-            loop(CHUNKS, lambda j: e_r(0, j).start())
-
-        @when(p == 3)
-        def _():
-            loop(CHUNKS, lambda j: e_l(3, CHUNKS - 1 - j).start())
-
-        hop(1)
-
-        @when(p == 1)
-        def _():
-            def one(j):
-                e_r(1, j).start()
-                e_r(0, j).wait_recv()
-                e_r(0, j).start()
-
-            loop(CHUNKS, one)
-
-        @when(p == 2)
-        def _():
-            def one(i):
-                j = CHUNKS - 1 - i
-                e_l(2, j).start()
-                e_l(3, j).wait_recv()
-                e_l(3, j).start()
-
-            loop(CHUNKS, one)
-
-        hop(2)
-
-        @when(p == 1)
-        def _():
-            def one(i):
-                j = CHUNKS - 1 - i
-                e_l(1, j).start()
-                e_l(2, j).wait_recv()
-                e_l(2, j).start()
-                e_l(3, j).wait_recv()
-                e_l(3, j).start()
-
-            loop(CHUNKS, one)
-
-        @when(p == 2)
-        def _():
-            def one(j):
-                e_r(2, j).start()
-                e_r(1, j).wait_recv()
-                e_r(1, j).start()
-                e_r(0, j).wait_recv()
-                e_r(0, j).start()
-
-            loop(CHUNKS, one)
 
         def nth(i):
             return jnp.where(p == 0, CHUNKS - 1 - i, i)
@@ -334,46 +453,264 @@
             im = (dot(ar, bi) + dot(ai, br)).astype(bf16)
             return re, im
 
-        @when(edge)
-        def _():
-            def one(i):
-                j = nth(i)
-
-                @when(p == 0)
-                def _():
-                    loop(PANELS - 1, lambda q: e_l(q + 1, j).wait_recv())
-
-                @when(p == 3)
-                def _():
-                    loop(PANELS - 1, lambda q: e_r(q, j).wait_recv())
-
-                def block(q):
-                    here = pl.ds(pl.multiple_of(q * rows, rows), rows)
-                    re, im = product(q, j)
-                    dsend[j, 0, here, :] = re
-                    dsend[j, 1, here, :] = im
-
+        def two(j, part):
+            return jnp.concatenate([ebuf[j, part], ebuf[j + 1, part]], axis=1)
+
+        def rows_of(q, j):
+            here = pl.ds(pl.multiple_of(q * rows, rows), rows)
+            ar, ai = obuf[0, here, :], obuf[1, here, :]
+            br, bi = two(j, 0), two(j, 1)
+            re = (dot(ar, br) - dot(ai, bi)).astype(bf16)
+            im = (dot(ar, bi) + dot(ai, br)).astype(bf16)
+            for n in range(2):
+                dsend[j + n, 0, here, :] = re[:, n * cols : (n + 1) * cols]
+                dsend[j + n, 1, here, :] = im[:, n * cols : (n + 1) * cols]
+
+        def e_in_chunk(j):
+            @when(p == 0)
+            def _():
+                loop(PANELS - 1, lambda q: e_l(q + 1, j).wait_recv())
+
+            @when(p == 3)
+            def _():
+                loop(PANELS - 1, lambda q: e_r(q, j).wait_recv())
+
+        def copy_own(j):
+            mine = pl.ds(pl.multiple_of(p * rows, rows), rows)
+            dloc[:, :, pl.ds(pl.multiple_of(j * cols, cols), cols)] = dsend[j, :, mine, :]
+
+        def own_chunk(j):
+            columns = pl.ds(pl.multiple_of(j * cols, cols), cols)
+            re, im = product(p, j)
+            dloc[0, :, columns] = re
+            dloc[1, :, columns] = im
+
+        def whole_chunk(i):
+            j = nth(i)
+            e_in_chunk(j)
+
+            def block(q):
+                here = pl.ds(pl.multiple_of(q * rows, rows), rows)
+                re, im = product(q, j)
+                dsend[j, 0, here, :] = re
+                dsend[j, 1, here, :] = im
+
+            @when(i < direct_out)
+            def _():
                 loop(PANELS, block)
 
-                @when((i < direct_out) & (site < sites - 1))
+                @when(site < sites - 1)
                 def _():
                     d_next(j).start()
 
-                mine = pl.ds(pl.multiple_of(p * rows, rows), rows)
-                columns = pl.ds(pl.multiple_of(j * cols, cols), cols)
-                dloc[:, :, columns] = dsend[j, :, mine, :]
-
-            loop(CHUNKS, one)
+                copy_own(j)
+
+            @when(i >= direct_out)
+            def _():
+                own_chunk(j)
+
+        @when(~odd)
+        def _():
+            loop(BANDS, lambda c: pass_o(p, c, True, True))
+            hop(0)
+            own_e()
+
+            @when(p == 0)
+            def _():
+                loop(CHUNKS, lambda j: e_r(0, j).start())
+
+            @when(p == 3)
+            def _():
+                loop(CHUNKS, lambda j: e_l(3, CHUNKS - 1 - j).start())
+
+            hop(1)
+
+            @when(p == 1)
+            def _():
+                def one(j):
+                    e_r(1, j).start()
+                    e_r(0, j).wait_recv()
+                    e_r(0, j).start()
+
+                loop(CHUNKS, one)
+
+            @when(p == 2)
+            def _():
+                def one(i):
+                    j = CHUNKS - 1 - i
+                    e_l(2, j).start()
+                    e_l(3, j).wait_recv()
+                    e_l(3, j).start()
+
+                loop(CHUNKS, one)
+
+            hop(2)
+
+            @when(p == 1)
+            def _():
+                def one(i):
+                    j = CHUNKS - 1 - i
+                    e_l(1, j).start()
+                    e_l(2, j).wait_recv()
+                    e_l(2, j).start()
+                    e_l(3, j).wait_recv()
+                    e_l(3, j).start()
+
+                loop(CHUNKS, one)
+
+            @when(p == 2)
+            def _():
+                def one(j):
+                    e_r(2, j).start()
+                    e_r(1, j).wait_recv()
+                    e_r(1, j).start()
+                    e_r(0, j).wait_recv()
+                    e_r(0, j).start()
+
+                loop(CHUNKS, one)
+
+            @when(edge)
+            def _():
+                loop(CHUNKS, whole_chunk)
+
+        def pair(q, j, sems, panel):
+            view = ebuf.at[pl.ds(j, 2), :, pl.ds(pl.multiple_of(q * rows, rows), rows), :]
+            return remote(view, view, sems.at[q, j], e_recv.at[q, j], at(0, panel))
+
+        def pair_r(q, b):
+            return pair(q, 2 * b, e_right, lax.rem(p + 1, PANELS))
+
+        def pair_l(q, b):
+            return pair(q, CHUNKS - 2 - 2 * b, e_left, lax.rem(p + PANELS - 1, PANELS))
+
+        sent = jnp.where(p == 0, 1, 0)
+
+        @when(odd)
+        def _():
+            def pass_e(q, b, right, left):
+                @when(right & (p < PANELS - 1))
+                def _():
+                    pair_r(q, b).start()
+
+                @when(left & (p > 0))
+                def _():
+                    pair_l(q, b).start()
+
+            def own_o(n):
+                def one(c):
+                    @when((p == n) & (p < PANELS - 1))
+                    def _():
+                        o_r(p, c).start()
+
+                    @when((p == PANELS - 1 - n) & (p > 0))
+                    def _():
+                        o_l(p, c).start()
+
+                loop(BANDS, one)
+
+            @when(site < sites - 2)
+            def _():
+                loop(BANDS, lambda c: o_up(p, c).start())
+
+            own_e()
+            for b in range(EARLY // 2):
+                pass_e(p, b, True, True)
+            own_o(0)
+            for n in range(PANELS - 1):
+                def one(b):
+                    @when(p - 1 - n >= 0)
+                    def _():
+                        pair_r(p - 1 - n, b).wait_recv()
+                        pass_e(p - 1 - n, b, True, False)
+
+                    @when(p + 1 + n < PANELS)
+                    def _():
+                        pair_l(p + 1 + n, b).wait_recv()
+                        pass_e(p + 1 + n, b, False, True)
+
+                loop(EARLY // 2, one)
+                own_o(n + 1)
+
+            def send_rows(k):
+                @when(edge)
+                def _():
+                    for g in range(2):
+                        rows_of(jnp.where(p == 0, k, PANELS - 1 - k), jnp.where(p == 0, CHUNKS - 2 - 2 * g, 2 * g))
+
+                        @when(site < sites - 1)
+                        def _():
+                            rows_next(sent, g, k).start()
+
+            send_rows(0)
+            hop(0)
+            send_rows(1)
+
+            @when(p == 0)
+            def _():
+                loop(EARLY, lambda i: e_r(0, EARLY + i).start())
+
+            @when(p == 3)
+            def _():
+                loop(EARLY, lambda i: e_l(3, EARLY - 1 - i).start())
+
+            hop(1)
+            send_rows(2)
+
+            @when(p == 1)
+            def _():
+                def one(i):
+                    j = EARLY + i
+                    e_r(1, j).start()
+                    e_r(0, j).wait_recv()
+                    e_r(0, j).start()
+
+                loop(EARLY, one)
+
+            @when(p == 2)
+            def _():
+                def one(i):
+                    j = EARLY - 1 - i
+                    e_l(2, j).start()
+                    e_l(3, j).wait_recv()
+                    e_l(3, j).start()
+
+                loop(EARLY, one)
+
+            hop(2)
+            send_rows(3)
+
+            @when(p == 1)
+            def _():
+                def one(i):
+                    j = EARLY - 1 - i
+                    e_l(1, j).start()
+                    e_l(2, j).wait_recv()
+                    e_l(2, j).start()
+                    e_l(3, j).wait_recv()
+                    e_l(3, j).start()
+
+                loop(EARLY, one)
+
+            @when(p == 2)
+            def _():
+                def one(i):
+                    j = EARLY + i
+                    e_r(2, j).start()
+                    e_r(1, j).wait_recv()
+                    e_r(1, j).start()
+                    e_r(0, j).wait_recv()
+                    e_r(0, j).start()
+
+                loop(EARLY, one)
+
+            @when(edge)
+            def _():
+                loop(EARLY, lambda i: whole_chunk(EARLY + i))
+                loop(EARLY, lambda i: copy_own(nth(i)))
 
         @when(~edge)
         def _():
-            def one(j):
-                columns = pl.ds(pl.multiple_of(j * cols, cols), cols)
-                re, im = product(p, j)
-                dloc[0, :, columns] = re
-                dloc[1, :, columns] = im
-
-            loop(CHUNKS, one)
+            loop(CHUNKS, own_chunk)
 
         def step(i):
             _, j = arrival(i)
@@ -390,7 +727,22 @@
         def _():
             out_ref[...] = dloc[...]
 
-        @when(site > 0)
+        def step_pair(i):
+            g = pick(i, (0, 1, 3, 2))
+            j = jnp.where(low, 2 * g, CHUNKS - 2 - 2 * g)
+            loop(2, lambda n: d_over(j + n).wait_recv())
+            columns = pl.ds(pl.multiple_of(j * cols, cols), 2 * cols)
+            ar, ai = dloc[0], dloc[1]
+            br = jnp.concatenate([drecv[j, 0], drecv[j + 1, 0]], axis=1)
+            bi = jnp.concatenate([drecv[j, 1], drecv[j + 1, 1]], axis=1)
+            out_ref[0, :, columns] = (dot(ar, br) - dot(ai, bi)).astype(bf16)
+            out_ref[1, :, columns] = (dot(ar, bi) + dot(ai, br)).astype(bf16)
+
+        @when((site > 0) & ~odd)
+        def _():
+            loop(CHUNKS // 2, step_pair)
+
+        @when((site > 0) & odd)
         def _():
             loop(CHUNKS, step)
 
@@ -416,22 +768,39 @@
 
             @when((q <= p) & (p < PANELS - 1))
             def _():
-                e_r(q, j).wait_send()
+                @when(~odd | (j >= EARLY))
+                def _():
+                    e_r(q, j).wait_send()
+
+                @when(odd & (j < EARLY // 2))
+                def _():
+                    pair_r(q, j).wait_send()
 
             @when((q >= p) & (p > 0))
             def _():
-                e_l(q, j).wait_send()
+                @when(~odd | (j < EARLY))
+                def _():
+                    e_l(q, j).wait_send()
+
+                @when(odd & (j >= EARLY) & (j < EARLY + EARLY // 2))
+                def _():
+                    pair_l(q, j - EARLY).wait_send()
 
         loop(PANELS * CHUNKS, drain_e)
 
         @when(edge)
         def _():
             def drain_d(i):
-                @when((i < direct_out) & (site < sites - 1))
+                @when((i < direct_out) & (site < sites - 1) & (~odd | (i >= EARLY)))
                 def _():
                     d_next(nth(i)).wait_send()
 
             loop(CHUNKS, drain_d)
+
+            @when(odd & (site < sites - 1))
+            def _():
+                for g in range(2):
+                    loop(PANELS, lambda k: rows_next(sent, g, k).wait_send())
 
 
 def shards(forward_props):
@@ -468,9 +837,14 @@
             dma((CHUNKS,)),
             dma((CHUNKS,)),
             dma((CHUNKS,)),
+            pltpu.VMEM(x.shape, bf16),
+            dma((BANDS,)),
+            dma((BANDS,)),
+            dma((2, 2 * PANELS)),
+            dma((2, 2 * PANELS)),
         ],
         compiler_params=pltpu.CompilerParams(
-            collective_id=0, has_side_effects=True, vmem_limit_bytes=48 * 2**20
+            collective_id=0, has_side_effects=True, vmem_limit_bytes=52 * 2**20
         ),
         name="prefix_products",
     )(x)

time: 103 us -> 99.8 us (0.969)
  Pallas kernels: 101 us -> 98.7 us
  local copies, waits for them, and re-layouts: 2.2 us -> 0.97 us
    pallas_call x1, Pallas kernels: 101 us -> 98.7 us  [shards(): pl.pallas_call(functools.partial(kernel, tm_size), out_shape=jax.ShapeDty...]
    unnamed x3 -> x1, local copies, waits for them, and re-layouts: 2.2 us -> 0.97 us
where the time goes in v4:
time: 99.8 us; the launch traced here: 99.6 us
  Pallas kernels  98.7 us (99%)
    pallas_call x1, Pallas kernels, shards(): pl.pallas_call(functools.partial(kernel, tm_size), out_shape=jax.ShapeDty...  98.7 us

profile of v4, /device:TPU:7, one launch (start us, length us, event | category | flops | bytes accessed | tf_op | source)
XLA Modules:
  0.0 99.6 jit_solution(17892558027582133064)
XLA Ops:
  0.0 98.7 %prefix_products.1 = bf16[2,256,1024]{2,1,0:T(8,128)(2,1)S(1)} custom-call(bf16[2,256,1024]{2,1,0:T(8,128)(2,1)} %bitcast.5), custom_call_target="tpu_custom_call" | custom-call | tf_op jit(solution)/shard_map/prefix_products/pallas_call | solution.py:812
  98.7 1.0 copy.4

commit v5 on v4

--- a/solution.py
+++ b/solution.py
@@ -34,7 +34,7 @@
 def kernel(
     tm_size, x_ref, out_ref, own, obuf, o2buf, ebuf, dsend, drecv, dloc, gbuf, acc,
     in_sem, o_recv, o_right, o_left, o_z, o2_recv, e_recv, e_right, e_left, e_in, d_recv, d_out, d_in,
-    relay, relay_recv, relay_out, rows_recv, rows_out,
+    relay, relay_recv, relay_out, rows_recv, rows_out, wide,
 ):
     rows, width = x_ref.shape[1], x_ref.shape[2]
     cols = width // CHUNKS
@@ -94,8 +94,17 @@
         return e_copy(q, j, e_left, lax.rem(p + PANELS - 1, PANELS))
 
     def e_over(j):
-        columns = pl.ds(pl.multiple_of(j * cols, cols), cols)
-        return remote(own.at[:, :, columns], e_piece(p, j), e_in.at[j], e_recv.at[p, j], at(1, p))
+        return remote(e_piece(p, j), e_piece(p, j), e_in.at[j], e_recv.at[p, j], at(1, p))
+
+    def pair(q, j, sems, shift, panel):
+        view = ebuf.at[pl.ds(j, 2), :, pl.ds(pl.multiple_of(q * rows, rows), rows), :]
+        return remote(view, view, sems.at[q, j], e_recv.at[q, j], at(shift, panel))
+
+    def pair_r(q, b, shift=0):
+        return pair(q, 2 * b, e_right, shift, lax.rem(p + 1, PANELS))
+
+    def pair_l(q, b, shift=0):
+        return pair(q, CHUNKS - 2 - 2 * b, e_left, shift, lax.rem(p + PANELS - 1, PANELS))
 
     def d_next(j):
         return remote(dsend.at[j], drecv.at[j], d_out.at[j], d_recv.at[j], at(1, PANELS - 1 - p))
@@ -151,9 +160,20 @@
         back = jnp.where(low, 0, PANELS - 1)
         return jnp.where(~edge & (a >= direct_in), back, onward)
 
-    load_e = pltpu.make_async_copy(x_ref, own, in_sem)
-    load_o = pltpu.make_async_copy(x_ref, obuf.at[:, pl.ds(pl.multiple_of(p * rows, rows), rows), :], in_sem)
-    when(core == 0)(load_e.start)
+    def load_chunk(j):
+        columns = pl.ds(pl.multiple_of(j * cols, cols), cols)
+        return pltpu.make_async_copy(x_ref.at[:, :, columns], e_piece(p, j), in_sem.at[j])
+
+    load_e = pltpu.make_async_copy(x_ref, own, in_sem.at[CHUNKS])
+    load_o = pltpu.make_async_copy(
+        x_ref, obuf.at[:, pl.ds(pl.multiple_of(p * rows, rows), rows), :], in_sem.at[CHUNKS]
+    )
+
+    @when(core == 0)
+    def _():
+        loop(CHUNKS, lambda j: load_chunk(j).start())
+        load_e.start()
+
     when(core == 1)(load_o.start)
 
     barrier = pltpu.get_barrier_semaphore()
@@ -189,12 +209,34 @@
     def _():
         greet(at(-1, p))
 
-    when(core == 0)(load_e.wait)
-    when(core == 1)(load_o.wait)
-    pl.semaphore_wait(barrier, jnp.where(edge & ~odd, jnp.where(core == 0, 2, 4), 3))
+        @when(odd & (p > 0))
+        def _():
+            greet(at(-1, p - 1))
+
+        @when(odd & (p < PANELS - 1))
+        def _():
+            greet(at(-1, p + 1))
+
 
     @when(core == 0)
     def _():
+        loop(CHUNKS, lambda j: load_chunk(j).wait())
+        load_e.wait()
+
+    when(core == 1)(load_o.wait)
+    heard = jnp.where(edge & ~odd, jnp.where(core == 0, 2, 4), 3)
+    pl.semaphore_wait(barrier, heard + jnp.where((core == 0) & odd, jnp.where(edge, 1, 2), 0))
+
+    @when(core == 0)
+    def _():
+        @when(odd & (p < PANELS - 1))
+        def _():
+            loop(EARLY // 2, lambda b: pair_r(p, b, 1).start())
+
+        @when(odd & (p > 0))
+        def _():
+            loop(EARLY // 2, lambda b: pair_l(p, b, 1).start())
+
         loop(CHUNKS, lambda j: e_over(j).start())
         acc[...] = jnp.zeros_like(acc)
 
@@ -214,19 +256,22 @@
             a, j = arrival(i)
             d_over(j).wait_recv()
 
-            @when(passes(a))
+            @when(passes(a) & ~held(a))
             def _():
                 d_pass(j, pass_to(a)).start()
 
             d_over(j).start()
+
+        def held(a):
+            return odd & ~edge & (a == 7)
 
         def multiply(i):
             _, j = arrival(i)
             columns = pl.ds(pl.multiple_of(j * cols, cols), cols)
-            er, ei = own[0], own[1]
             dr, di = drecv[j, 0], drecv[j, 1]
-            gbuf[0, :, columns] = (dot(er, dr) - dot(ei, di)).astype(bf16)
-            gbuf[1, :, columns] = (dot(er, di) + dot(ei, dr)).astype(bf16)
+            both = dot(own[0], jnp.concatenate([dr, di], axis=1)) + dot(own[1], jnp.concatenate([-di, dr], axis=1))
+            gbuf[0, :, columns] = both[:, :cols].astype(bf16)
+            gbuf[1, :, columns] = both[:, cols:].astype(bf16)
 
         def add(i, final=False):
             _, j = arrival(i)
@@ -237,9 +282,9 @@
             loop(BANDS // 2, rows_in)
             columns = pl.ds(pl.multiple_of(j * cols, cols), cols)
             gr, gi = gbuf[0, :, columns], gbuf[1, :, columns]
-            tr, ti = o2buf[0, columns, :], o2buf[1, columns, :]
-            re = acc[0] + (dot(gr, tr) - dot(gi, ti))
-            im = acc[1] + (dot(gr, ti) + dot(gi, tr))
+            below = jnp.concatenate([o2buf[0, columns, :], o2buf[1, columns, :]], axis=0)
+            re = acc[0] + dot(jnp.concatenate([gr, -gi], axis=1), below)
+            im = acc[1] + dot(jnp.concatenate([gi, gr], axis=1), below)
             if final:
                 out_ref[0] = re.astype(bf16)
                 out_ref[1] = im.astype(bf16)
@@ -280,6 +325,10 @@
         def step(i):
             take(i)
 
+            @when(odd & ~edge & (i == 5))
+            def _():
+                d_pass(jnp.where(low, 7, 0), pass_to(7)).start()
+
             def more(n, carry):
                 add(n)
                 return carry
@@ -399,6 +448,14 @@
                 d_pass(arrival(4)[1], 1).wait_send()
 
         loop(CHUNKS, lambda j: e_over(j).wait_send())
+
+        @when(odd & (p < PANELS - 1))
+        def _():
+            loop(EARLY // 2, lambda b: pair_r(p, b, 1).wait_send())
+
+        @when(odd & (p > 0))
+        def _():
+            loop(EARLY // 2, lambda b: pair_l(p, b, 1).wait_send())
 
         @when(edge & odd & (site > 2))
         def _():
@@ -491,12 +548,14 @@
 
             def block(q):
                 here = pl.ds(pl.multiple_of(q * rows, rows), rows)
-                re, im = product(q, j)
-                dsend[j, 0, here, :] = re
-                dsend[j, 1, here, :] = im
+                both = (dot(obuf[0, here, :], wide[0]) + dot(obuf[1, here, :], wide[1])).astype(bf16)
+                dsend[j, 0, here, :] = both[:, :cols]
+                dsend[j, 1, here, :] = both[:, cols:]
 
             @when(i < direct_out)
             def _():
+                wide[0] = jnp.concatenate([ebuf[j, 0], ebuf[j, 1]], axis=1)
+                wide[1] = jnp.concatenate([-ebuf[j, 1], ebuf[j, 0]], axis=1)
                 loop(PANELS, block)
 
                 @when(site < sites - 1)
@@ -573,16 +632,6 @@
             def _():
                 loop(CHUNKS, whole_chunk)
 
-        def pair(q, j, sems, panel):
-            view = ebuf.at[pl.ds(j, 2), :, pl.ds(pl.multiple_of(q * rows, rows), rows), :]
-            return remote(view, view, sems.at[q, j], e_recv.at[q, j], at(0, panel))
-
-        def pair_r(q, b):
-            return pair(q, 2 * b, e_right, lax.rem(p + 1, PANELS))
-
-        def pair_l(q, b):
-            return pair(q, CHUNKS - 2 - 2 * b, e_left, lax.rem(p + PANELS - 1, PANELS))
-
         sent = jnp.where(p == 0, 1, 0)
 
         @when(odd)
@@ -612,10 +661,6 @@
             def _():
                 loop(BANDS, lambda c: o_up(p, c).start())
 
-            own_e()
-            for b in range(EARLY // 2):
-                pass_e(p, b, True, True)
-            own_o(0)
             for n in range(PANELS - 1):
                 def one(b):
                     @when(p - 1 - n >= 0)
@@ -629,6 +674,8 @@
                         pass_e(p + 1 + n, b, False, True)
 
                 loop(EARLY // 2, one)
+                if n == 0:
+                    own_o(0)
                 own_o(n + 1)
 
             def send_rows(k):
@@ -641,6 +688,7 @@
                         def _():
                             rows_next(sent, g, k).start()
 
+            own_e()
             send_rows(0)
             hop(0)
             send_rows(1)
@@ -716,10 +764,9 @@
             _, j = arrival(i)
             d_over(j).wait_recv()
             columns = pl.ds(pl.multiple_of(j * cols, cols), cols)
-            ar, ai = dloc[0], dloc[1]
             br, bi = drecv[j, 0], drecv[j, 1]
-            re = (dot(ar, br) - dot(ai, bi)).astype(bf16)
-            im = (dot(ar, bi) + dot(ai, br)).astype(bf16)
+            both = dot(dloc[0], jnp.concatenate([br, bi], axis=1)) + dot(dloc[1], jnp.concatenate([-bi, br], axis=1))
+            re, im = both[:, :cols].astype(bf16), both[:, cols:].astype(bf16)
             out_ref[0, :, columns] = re
             out_ref[1, :, columns] = im
 
@@ -772,7 +819,7 @@
                 def _():
                     e_r(q, j).wait_send()
 
-                @when(odd & (j < EARLY // 2))
+                @when(odd & (q < p) & (j < EARLY // 2))
                 def _():
                     pair_r(q, j).wait_send()
 
@@ -782,7 +829,7 @@
                 def _():
                     e_l(q, j).wait_send()
 
-                @when(odd & (j >= EARLY) & (j < EARLY + EARLY // 2))
+                @when(odd & (q > p) & (j >= EARLY) & (j < EARLY + EARLY // 2))
                 def _():
                     pair_l(q, j - EARLY).wait_send()
 
@@ -824,7 +871,7 @@
             pltpu.VMEM(x.shape, bf16),
             pltpu.VMEM(x.shape, bf16),
             pltpu.VMEM(x.shape, f32),
-            dma,
+            dma((CHUNKS + 1,)),
             dma((PANELS, BANDS)),
             dma((PANELS, BANDS)),
             dma((PANELS, BANDS)),
@@ -842,6 +889,7 @@
             dma((BANDS,)),
             dma((2, 2 * PANELS)),
             dma((2, 2 * PANELS)),
+            pltpu.VMEM((2, width, 2 * cols), bf16),
         ],
         compiler_params=pltpu.CompilerParams(
             collective_id=0, has_side_effects=True, vmem_limit_bytes=52 * 2**20

time: 99.8 us -> 98 us (0.982)
  Pallas kernels: 98.7 us -> 96.9 us
    pallas_call x1, Pallas kernels: 98.7 us -> 96.9 us  [shards(): pl.pallas_call(functools.partial(kernel, tm_size), out_shape=jax.ShapeDty...]
where the time goes in v5:
time: 98 us; the launch traced here: 97.9 us
  Pallas kernels  96.9 us (99%)
    pallas_call x1, Pallas kernels, shards(): pl.pallas_call(functools.partial(kernel, tm_size), out_shape=jax.ShapeDty...  96.9 us

profile of v5, /device:TPU:7, one launch (start us, length us, event | category | flops | bytes accessed | tf_op | source)
XLA Modules:
  0.0 97.9 jit_solution(13013724585219765621)
XLA Ops:
  0.0 96.9 %prefix_products.1 = bf16[2,256,1024]{2,1,0:T(8,128)(2,1)S(1)} custom-call(bf16[2,256,1024]{2,1,0:T(8,128)(2,1)} %bitcast.5), custom_call_target="tpu_custom_call" | custom-call | tf_op jit(solution)/shard_map/prefix_products/pallas_call | solution.py:859
  96.9 1.0 copy.4

commit v6 on v5

--- a/solution.py
+++ b/solution.py
@@ -9,6 +9,7 @@
 
 PANELS = 4
 CHUNKS = 8
+HELD = 2
 EARLY = 4
 BANDS = 4
 
@@ -221,7 +222,6 @@
     @when(core == 0)
     def _():
         loop(CHUNKS, lambda j: load_chunk(j).wait())
-        load_e.wait()
 
     when(core == 1)(load_o.wait)
     heard = jnp.where(edge & ~odd, jnp.where(core == 0, 2, 4), 3)
@@ -238,6 +238,7 @@
             loop(EARLY // 2, lambda b: pair_l(p, b, 1).start())
 
         loop(CHUNKS, lambda j: e_over(j).start())
+        load_e.wait()
         acc[...] = jnp.zeros_like(acc)
 
         @when(edge & odd & (site > 2))
@@ -351,16 +352,19 @@
         def span(first, end, f):
             loop(end - first, lambda i: f(first + i))
 
+        def give_back(k):
+            def one(n, carry):
+                rows_pass(other, 0, n, 2, pass_to(7)).start()
+                return carry
+
+            lax.fori_loop(jnp.where(k == HELD, 0, k), jnp.where(k < HELD, k, k + 1), one, 0)
+
         def take_rows(k):
             @when(edge)
             def _():
                 for g in range(2):
                     rows_pass(main, g, k, 2, pass_to(0)).wait_recv()
                     rows_pass(main, g, k, 2, pass_to(0)).start()
-
-                @when(k > 0)
-                def _():
-                    rows_pass(other, 0, k - 1, 2, pass_to(0)).wait_recv()
 
             @when(~edge)
             def _():
@@ -370,7 +374,7 @@
                 for g in range(2):
                     rows_pass(other, g, k, 2 - g, pass_to(0)).wait_recv()
                     if g == 0:
-                        rows_pass(other, g, k, 2, pass_to(7)).start()
+                        give_back(k)
 
         def drain_rows(k):
             rows_pass(main, 0, k, 2, pass_to(0)).wait_send()
@@ -387,6 +391,20 @@
         def over(i):
             d_over(arrival(i)[1]).start()
 
+        loop(CHUNKS, lambda j: e_over(j).wait_send())
+
+        @when(odd & (p < PANELS - 1))
+        def _():
+            loop(EARLY // 2, lambda b: pair_r(p, b, 1).wait_send())
+
+        @when(odd & (p > 0))
+        def _():
+            loop(EARLY // 2, lambda b: pair_l(p, b, 1).wait_send())
+
+        @when(edge & odd & (site > 2))
+        def _():
+            loop(BANDS, lambda c: o_aside_on(c).wait_send())
+
         @when(site == 0)
         def _():
             out_ref[...] = own[...]
@@ -411,22 +429,23 @@
             def _():
                 come(4)
                 loop(2, add_pair)
-                rows_pass(other, 0, PANELS - 1, 2, pass_to(0)).wait_recv()
+                loop(PANELS, lambda k: rows_pass(other, 0, k, 2, pass_to(0)).wait_recv())
                 span(5, 7, over)
+                come(7)
 
             multiply_pair(3)
 
             @when(~edge)
             def _():
+                loop(2, add_pair)
+
+            add_pair(3)
+
+            @when(~edge)
+            def _():
                 come(7)
-                loop(2, add_pair)
-
-            add_pair(3)
-
-            @when(edge)
-            def _():
-                come(7)
-
+
+            loop(PANELS, drain_rows)
             multiply_pair(2)
             add_pair(2, final=True)
 
@@ -440,26 +459,11 @@
 
         @when((site > 0) & ~odd)
         def _():
-            loop(PANELS, drain_rows)
             loop(CHUNKS, lambda j: d_over(j).wait_send())
 
             @when(edge)
             def _():
                 d_pass(arrival(4)[1], 1).wait_send()
-
-        loop(CHUNKS, lambda j: e_over(j).wait_send())
-
-        @when(odd & (p < PANELS - 1))
-        def _():
-            loop(EARLY // 2, lambda b: pair_r(p, b, 1).wait_send())
-
-        @when(odd & (p > 0))
-        def _():
-            loop(EARLY // 2, lambda b: pair_l(p, b, 1).wait_send())
-
-        @when(edge & odd & (site > 2))
-        def _():
-            loop(BANDS, lambda c: o_aside_on(c).wait_send())
 
     @when(core == 1)
     def _():
@@ -760,6 +764,48 @@
         def _():
             loop(CHUNKS, own_chunk)
 
+        def drain_o(i):
+            q, c = i // BANDS, lax.rem(i, BANDS)
+
+            @when(site < sites - 2)
+            def _():
+                o_up(q, c).wait_send()
+
+            @when((q <= p) & (p < PANELS - 1))
+            def _():
+                o_r(q, c).wait_send()
+
+            @when((q >= p) & (p > 0))
+            def _():
+                o_l(q, c).wait_send()
+
+        loop(PANELS * BANDS, drain_o)
+
+        def drain_e(i):
+            q, j = i // CHUNKS, lax.rem(i, CHUNKS)
+
+            @when((q <= p) & (p < PANELS - 1))
+            def _():
+                @when(~odd | (j >= EARLY))
+                def _():
+                    e_r(q, j).wait_send()
+
+                @when(odd & (q < p) & (j < EARLY // 2))
+                def _():
+                    pair_r(q, j).wait_send()
+
+            @when((q >= p) & (p > 0))
+            def _():
+                @when(~odd | (j < EARLY))
+                def _():
+                    e_l(q, j).wait_send()
+
+                @when(odd & (q > p) & (j >= EARLY) & (j < EARLY + EARLY // 2))
+                def _():
+                    pair_l(q, j - EARLY).wait_send()
+
+        loop(PANELS * CHUNKS, drain_e)
+
         def step(i):
             _, j = arrival(i)
             d_over(j).wait_recv()
@@ -769,6 +815,21 @@
             re, im = both[:, :cols].astype(bf16), both[:, cols:].astype(bf16)
             out_ref[0, :, columns] = re
             out_ref[1, :, columns] = im
+
+        def drain_sent():
+            def drain_d(i):
+                @when((i < direct_out) & (site < sites - 1) & (~odd | (i >= EARLY)))
+                def _():
+                    d_next(nth(i)).wait_send()
+
+            loop(CHUNKS, drain_d)
+
+            @when(odd & (site < sites - 1))
+            def _():
+                for g in range(2):
+                    loop(PANELS, lambda k: rows_next(sent, g, k).wait_send())
+
+        when(edge & odd)(drain_sent)
 
         @when(site == 0)
         def _():
@@ -793,61 +854,7 @@
         def _():
             loop(CHUNKS, step)
 
-        def drain_o(i):
-            q, c = i // BANDS, lax.rem(i, BANDS)
-
-            @when(site < sites - 2)
-            def _():
-                o_up(q, c).wait_send()
-
-            @when((q <= p) & (p < PANELS - 1))
-            def _():
-                o_r(q, c).wait_send()
-
-            @when((q >= p) & (p > 0))
-            def _():
-                o_l(q, c).wait_send()
-
-        loop(PANELS * BANDS, drain_o)
-
-        def drain_e(i):
-            q, j = i // CHUNKS, lax.rem(i, CHUNKS)
-
-            @when((q <= p) & (p < PANELS - 1))
-            def _():
-                @when(~odd | (j >= EARLY))
-                def _():
-                    e_r(q, j).wait_send()
-
-                @when(odd & (q < p) & (j < EARLY // 2))
-                def _():
-                    pair_r(q, j).wait_send()
-
-            @when((q >= p) & (p > 0))
-            def _():
-                @when(~odd | (j < EARLY))
-                def _():
-                    e_l(q, j).wait_send()
-
-                @when(odd & (q > p) & (j >= EARLY) & (j < EARLY + EARLY // 2))
-                def _():
-                    pair_l(q, j - EARLY).wait_send()
-
-        loop(PANELS * CHUNKS, drain_e)
-
-        @when(edge)
-        def _():
-            def drain_d(i):
-                @when((i < direct_out) & (site < sites - 1) & (~odd | (i >= EARLY)))
-                def _():
-                    d_next(nth(i)).wait_send()
-
-            loop(CHUNKS, drain_d)
-
-            @when(odd & (site < sites - 1))
-            def _():
-                for g in range(2):
-                    loop(PANELS, lambda k: rows_next(sent, g, k).wait_send())
+        when(edge & ~odd)(drain_sent)
 
 
 def shards(forward_props):

time: 98 us -> 96.6 us (0.986)
  Pallas kernels: 96.9 us -> 95.5 us
    pallas_call x1, Pallas kernels: 96.9 us -> 95.5 us  [shards(): pl.pallas_call(functools.partial(kernel, tm_size), out_shape=jax.ShapeDty...]
where the time goes in v6:
time: 96.6 us; the launch traced here: 96.4 us
  Pallas kernels  95.5 us (99%)
  local copies, waits for them, and re-layouts  0.97 us (1%)
    pallas_call x1, Pallas kernels, shards(): pl.pallas_call(functools.partial(kernel, tm_size), out_shape=jax.ShapeDty...  95.5 us

profile of v6, /device:TPU:7, one launch (start us, length us, event | category | flops | bytes accessed | tf_op | source)
XLA Modules:
  0.0 96.4 jit_solution(14538459419925581331)
XLA Ops:
  0.0 95.5 %prefix_products.1 = bf16[2,256,1024]{2,1,0:T(8,128)(2,1)S(1)} custom-call(bf16[2,256,1024]{2,1,0:T(8,128)(2,1)} %bitcast.5), custom_call_target="tpu_custom_call" | custom-call | tf_op jit(solution)/shard_map/prefix_products/pallas_call | solution.py:866
  95.5 1.0 %copy.4 = bf16[2,1,256,1024]{3,2,1,0:T(8,128)(2,1)} copy(bf16[2,1,256,1024]{3,2,1,0:T(8,128)(2,1)S(1)} %bitcast.4) | data formatting | bytes 2097152

commit v7 on v6

--- a/solution.py
+++ b/solution.py
@@ -9,7 +9,8 @@
 
 PANELS = 4
 CHUNKS = 8
-HELD = 2
+PIECES = 2 * PANELS
+HELD = 4
 EARLY = 4
 BANDS = 4
 
@@ -118,20 +119,22 @@
 
     def piece(half, g, k, n):
         first = 2 * g
-        q = jnp.where(half == 0, PANELS - 1 - k, k)
+        q = jnp.where(half == 0, PANELS - 1 - k // 2, k // 2)
         j = jnp.where(half == 0, first, CHUNKS - first - n)
-        return pl.ds(j, n), slice(None), pl.ds(pl.multiple_of(q * rows, rows), rows), slice(None)
+        part = rows // 2
+        start = pl.multiple_of(q * rows + lax.rem(k, 2) * part, part)
+        return pl.ds(j, n), slice(None), pl.ds(start, part), slice(None)
 
     def rows_next(half, g, k):
         view = piece(half, g, k, 2)
-        m = PANELS * g + k
+        m = PIECES * g + k
         return remote(
             dsend.at[view], drecv.at[view], rows_out.at[half, m], rows_recv.at[half, m], at(1, PANELS - 1 - p)
         )
 
     def rows_pass(half, g, k, n, panel):
         view = piece(half, g, k, n)
-        m = PANELS * g + k
+        m = PIECES * g + k
         return remote(drecv.at[view], drecv.at[view], rows_out.at[half, m], rows_recv.at[half, m], at(0, panel))
 
     odd = lax.rem(site, 2) == 1
@@ -416,7 +419,7 @@
 
         @when((site > 0) & ~odd)
         def _():
-            loop(PANELS, take_rows)
+            loop(PIECES, take_rows)
             span(0, 4, over)
 
             @when(~edge)
@@ -429,7 +432,7 @@
             def _():
                 come(4)
                 loop(2, add_pair)
-                loop(PANELS, lambda k: rows_pass(other, 0, k, 2, pass_to(0)).wait_recv())
+                loop(PIECES, lambda k: rows_pass(other, 0, k, 2, pass_to(0)).wait_recv())
                 span(5, 7, over)
                 come(7)
 
@@ -445,7 +448,7 @@
             def _():
                 come(7)
 
-            loop(PANELS, drain_rows)
+            loop(PIECES, drain_rows)
             multiply_pair(2)
             add_pair(2, final=True)
 
@@ -486,19 +489,19 @@
             def _():
                 o_aside(c).start()
 
+        def hop_band(n, c):
+            @when(p - 1 - n >= 0)
+            def _():
+                o_r(p - 1 - n, c).wait_recv()
+                pass_o(p - 1 - n, c, True, False)
+
+            @when(p + 1 + n < PANELS)
+            def _():
+                o_l(p + 1 + n, c).wait_recv()
+                pass_o(p + 1 + n, c, False, True)
+
         def hop(n):
-            def one(c):
-                @when(p - 1 - n >= 0)
-                def _():
-                    o_r(p - 1 - n, c).wait_recv()
-                    pass_o(p - 1 - n, c, True, False)
-
-                @when(p + 1 + n < PANELS)
-                def _():
-                    o_l(p + 1 + n, c).wait_recv()
-                    pass_o(p + 1 + n, c, False, True)
-
-            loop(BANDS, one)
+            loop(BANDS, lambda c: hop_band(n, c))
 
         def own_e():
             loop(CHUNKS, lambda j: e_over(j).wait_recv())
@@ -517,8 +520,8 @@
         def two(j, part):
             return jnp.concatenate([ebuf[j, part], ebuf[j + 1, part]], axis=1)
 
-        def rows_of(q, j):
-            here = pl.ds(pl.multiple_of(q * rows, rows), rows)
+        def rows_of(q, b, j):
+            here = pl.ds(pl.multiple_of(q * rows + b * (rows // 2), rows // 2), rows // 2)
             ar, ai = obuf[0, here, :], obuf[1, here, :]
             br, bi = two(j, 0), two(j, 1)
             re = (dot(ar, br) - dot(ai, bi)).astype(bf16)
@@ -685,17 +688,27 @@
             def send_rows(k):
                 @when(edge)
                 def _():
-                    for g in range(2):
-                        rows_of(jnp.where(p == 0, k, PANELS - 1 - k), jnp.where(p == 0, CHUNKS - 2 - 2 * g, 2 * g))
+                    def one(g):
+                        q = jnp.where(p == 0, k // 2, PANELS - 1 - k // 2)
+                        rows_of(q, lax.rem(k, 2), jnp.where(p == 0, CHUNKS - 2 - 2 * g, 2 * g))
 
                         @when(site < sites - 1)
                         def _():
-                            rows_next(sent, g, k).start()
+                            for n in range(2):
+                                when(g == n)(rows_next(sent, n, k).start)
+
+                    loop(2, one)
+
+            def hop_and_send(n):
+                def half(b):
+                    loop(BANDS // 2, lambda c: hop_band(n, b * (BANDS // 2) + c))
+                    send_rows(2 * n + 2 + b)
+
+                loop(2, half)
 
             own_e()
-            send_rows(0)
-            hop(0)
-            send_rows(1)
+            loop(2, send_rows)
+            hop_and_send(0)
 
             @when(p == 0)
             def _():
@@ -705,8 +718,7 @@
             def _():
                 loop(EARLY, lambda i: e_l(3, EARLY - 1 - i).start())
 
-            hop(1)
-            send_rows(2)
+            hop_and_send(1)
 
             @when(p == 1)
             def _():
@@ -728,8 +740,7 @@
 
                 loop(EARLY, one)
 
-            hop(2)
-            send_rows(3)
+            hop_and_send(2)
 
             @when(p == 1)
             def _():
@@ -827,7 +838,7 @@
             @when(odd & (site < sites - 1))
             def _():
                 for g in range(2):
-                    loop(PANELS, lambda k: rows_next(sent, g, k).wait_send())
+                    loop(PIECES, lambda k: rows_next(sent, g, k).wait_send())
 
         when(edge & odd)(drain_sent)
 
@@ -894,8 +905,8 @@
             pltpu.VMEM(x.shape, bf16),
             dma((BANDS,)),
             dma((BANDS,)),
-            dma((2, 2 * PANELS)),
-            dma((2, 2 * PANELS)),
+            dma((2, 2 * PIECES)),
+            dma((2, 2 * PIECES)),
             pltpu.VMEM((2, width, 2 * cols), bf16),
         ],
         compiler_params=pltpu.CompilerParams(

time: 96.6 us -> 95.4 us (0.988); the launches traced: 96.4 us -> 94.1 us
  Pallas kernels: 95.5 us -> 93.1 us
    pallas_call x1, Pallas kernels: 95.5 us -> 93.1 us  [shards(): pl.pallas_call(functools.partial(kernel, tm_size), out_shape=jax.ShapeDty...]
where the time goes in v7:
time: 95.4 us; the launch traced here: 94.1 us
  Pallas kernels  93.1 us (98%)
  local copies, waits for them, and re-layouts  0.97 us (1%)
    pallas_call x1, Pallas kernels, shards(): pl.pallas_call(functools.partial(kernel, tm_size), out_shape=jax.ShapeDty...  93.1 us

profile of v7, /device:TPU:7, one launch (start us, length us, event | category | flops | bytes accessed | tf_op | source)
XLA Modules:
  0.0 94.1 jit_solution(14588022831484464185)
XLA Ops:
  0.0 93.1 %prefix_products.1 = bf16[2,256,1024]{2,1,0:T(8,128)(2,1)S(1)} custom-call(bf16[2,256,1024]{2,1,0:T(8,128)(2,1)} %bitcast.5), custom_call_target="tpu_custom_call" | custom-call | tf_op jit(solution)/shard_map/prefix_products/pallas_call | solution.py:877
  93.1 1.0 %copy.4 = bf16[2,1,256,1024]{3,2,1,0:T(8,128)(2,1)} copy(bf16[2,1,256,1024]{3,2,1,0:T(8,128)(2,1)S(1)} %bitcast.4) | data formatting | bytes 2097152

commit v8 on v7

--- a/solution.py
+++ b/solution.py
@@ -10,7 +10,7 @@
 PANELS = 4
 CHUNKS = 8
 PIECES = 2 * PANELS
-HELD = 4
+GIVEN = (0, 0, 0, 0, 1, 3, 6, 8)
 EARLY = 4
 BANDS = 4
 
@@ -360,7 +360,7 @@
                 rows_pass(other, 0, n, 2, pass_to(7)).start()
                 return carry
 
-            lax.fori_loop(jnp.where(k == HELD, 0, k), jnp.where(k < HELD, k, k + 1), one, 0)
+            lax.fori_loop(pick(k, (0,) + GIVEN[:-1]), pick(k, GIVEN), one, 0)
 
         def take_rows(k):
             @when(edge)

time: 95.4 us -> 95.6 us (level); the launches traced: 94.1 us -> 95.5 us
  Pallas kernels: 93.1 us -> 94.5 us
    pallas_call x1, Pallas kernels: 93.1 us -> 94.5 us  [shards(): pl.pallas_call(functools.partial(kernel, tm_size), out_shape=jax.ShapeDty...]
where the time goes in v8:
time: 95.6 us; the launch traced here: 95.5 us
  Pallas kernels  94.5 us (99%)
  local copies, waits for them, and re-layouts  0.97 us (1%)
    pallas_call x1, Pallas kernels, shards(): pl.pallas_call(functools.partial(kernel, tm_size), out_shape=jax.ShapeDty...  94.5 us

profile of v8, /device:TPU:7, one launch (start us, length us, event | category | flops | bytes accessed | tf_op | source)
XLA Modules:
  0.0 95.5 jit_solution(17809736604470384171)
XLA Ops:
  0.0 94.5 %prefix_products.1 = bf16[2,256,1024]{2,1,0:T(8,128)(2,1)S(1)} custom-call(bf16[2,256,1024]{2,1,0:T(8,128)(2,1)} %bitcast.5), custom_call_target="tpu_custom_call" | custom-call | tf_op jit(solution)/shard_map/prefix_products/pallas_call | solution.py:877
  94.5 1.0 %copy.4 = bf16[2,1,256,1024]{3,2,1,0:T(8,128)(2,1)} copy(bf16[2,1,256,1024]{3,2,1,0:T(8,128)(2,1)S(1)} %bitcast.4) | data formatting | bytes 2097152
